TPU v7x, 128 devices: a whole 4x4x4 slice. The times are simulated.
128 devices in a mesh: dp: 16 (over x_hi, y, core), tensor: 8 (over z, x_lo).
Axes of the slice: x: 4 (x_hi: 2, x_lo: 2; x = x_hi * 2 + x_lo), y: 4, z: 4, core: 2. Of those that a mesh axis runs over, the one named last changes fastest.
Arguments:
- hidden: bfloat16 [2, 16, 512, 1536], P(None, 'dp', 'tensor'), may hold values from -6 to 6
- condition: bfloat16 [2, 16, 1024], P(None, 'dp'), may hold values from -6 to 6
- caption: bfloat16 [2, 16, 256, 4096], P(None, 'dp'), may hold values from -6 to 6
- lengths: int32 [2, 16], P(None, 'dp'), may hold values from 128 to 512, as said below
- frames: int32 [2, 16], P(None, 'dp'), may hold values from 1 to 4
- widths: int32 [2, 16], P(None, 'dp'), may hold values from 8 to 32
- caption_lens: int32 [2, 16], P(None, 'dp'), may hold values from 32 to 256, as said below
- cotangent: bfloat16 [2, 16, 512, 1536], P(None, 'dp', 'tensor'), may hold values from -6 to 6
- ada_weight: bfloat16 [1024, 6144], P('dp', 'tensor'), may hold values from -0.1875 to 0.1875
- ada_bias: bfloat16 [6144], P('dp'), may hold values from -3 to 3
- norm_gains: bfloat16 [4, 1536], P(None, 'dp'), may hold values from 0.25 to 1.75
- qkv_weight: bfloat16 [3, 1536, 1536], P(None, 'dp', 'tensor'), may hold values from -0.15625 to 0.15625
- head_gains: bfloat16 [3, 64], replicated, may hold values from 0.25 to 1.75
- caption_weight: bfloat16 [2, 4096, 1536], P(None, 'dp', 'tensor'), may hold values from -0.09375 to 0.09375
- head_gate: bfloat16 [24], replicated, may hold values from -1.5 to 1.5
- out_weight: bfloat16 [1536, 1536], P('tensor', 'dp'), may hold values from -0.15625 to 0.15625
- ffn_weight: bfloat16 [2, 1536, 4096], P(None, 'dp', 'tensor'), may hold values from -0.15625 to 0.15625
- down_weight: bfloat16 [4096, 1536], P('tensor', 'dp'), may hold values from -0.09375 to 0.09375
Outputs:
- layer_out: bfloat16 [2, 16, 512, 1536], P(None, 'dp', 'tensor')
- grad_hidden: float32 [2, 16, 512, 1536], P(None, 'dp', 'tensor')
- grad_ada_weight: float32 [1024, 6144], P('dp', 'tensor')
- grad_ada_bias: float32 [6144], P('dp')
- grad_norm_gains: float32 [4, 1536], P(None, 'dp')
- grad_qkv_weight: float32 [3, 1536, 1536], P(None, 'dp', 'tensor')
- grad_head_gains: float32 [3, 64], replicated
- grad_caption_weight: float32 [2, 4096, 1536], P(None, 'dp', 'tensor')
- grad_head_gate: float32 [24], replicated
- grad_out_weight: float32 [1536, 1536], P('tensor', 'dp')
- grad_ffn_weight: float32 [2, 1536, 4096], P(None, 'dp', 'tensor')
- grad_down_weight: float32 [4096, 1536], P('tensor', 'dp')
Inputs may be any that keep to these rules, and one draw needn't show every extreme that they name: `lengths`: for every item index, one of the 2 micro-batches holds an item with all 512 slots live. `caption_lens`: for every item index, one of the 2 micro-batches holds an item with all 256 caption slots live.
All inputs are finite; a program needn't handle non-finite values.
Results may differ from a plain program's by a relative error of at most 0.023.
Values may be sent and summed in bfloat16 or wider, within the bound.
A program may use at most 192 MiB of HBM per device.

v0:
```python
import jax
import jax.numpy as jnp
from jax import lax
from jax.sharding import PartitionSpec as P

H = 24
HD = 64


EPSILON = 1e-05
NEGATIVE = -1e30


def normalize(values):
    inverse = lax.rsqrt(jnp.mean(values * values, axis=-1, keepdims=True) + EPSILON)
    return (values * inverse, inverse)


def norm_back(unit_values, inverse, gradient):
    return inverse * (
        gradient - unit_values * jnp.mean(gradient * unit_values, axis=-1, keepdims=True)
    )


def swish(values):
    return values * jax.nn.sigmoid(values)


def rope_tables(length, frames, width, total, head_size):
    position = jnp.arange(total, dtype=jnp.int32)
    per_frame = (length + frames - 1) // frames
    frame_pos = position // per_frame
    within = position - frame_pos * per_frame
    row_pos = within // width
    col_pos = within - row_pos * width
    half_size = head_size // 2
    time_pairs = head_size // 8
    space_pairs = (half_size - time_pairs) // 2
    pair = jnp.arange(half_size, dtype=jnp.int32)
    in_row = pair >= time_pairs
    in_col = pair >= time_pairs + space_pairs
    offset = jnp.where(in_col, time_pairs + space_pairs, jnp.where(in_row, time_pairs, 0))
    group_size = jnp.where(in_row, space_pairs, time_pairs)
    freq = 10000.0 ** (-(pair - offset).astype(jnp.float32) / group_size.astype(jnp.float32))
    chosen = jnp.where(
        in_col[None, :],
        col_pos[:, None],
        jnp.where(in_row[None, :], row_pos[:, None], frame_pos[:, None]),
    )
    angle = chosen.astype(jnp.float32) * freq[None, :]
    return (jnp.cos(angle), jnp.sin(angle))


def rotate(values, cosine, sine_table):
    half_size = values.shape[-1] // 2
    first_half = values[..., :half_size]
    second_half = values[..., half_size:]
    cos_rows = cosine[:, None, :]
    sin_rows = sine_table[:, None, :]
    return jnp.concatenate(
        [
            first_half * cos_rows - second_half * sin_rows,
            first_half * sin_rows + second_half * cos_rows,
        ],
        axis=-1,
    )


def rotate_back(gradient, cosine, sine_table):
    half_size = gradient.shape[-1] // 2
    first_half = gradient[..., :half_size]
    second_half = gradient[..., half_size:]
    cos_rows = cosine[:, None, :]
    sin_rows = sine_table[:, None, :]
    return jnp.concatenate(
        [
            first_half * cos_rows + second_half * sin_rows,
            second_half * cos_rows - first_half * sin_rows,
        ],
        axis=-1,
    )


def softmax_parts(scores, live_keys):
    masked = jnp.where(live_keys[None, None, :], scores, NEGATIVE)
    top_score = jnp.max(masked, axis=-1, keepdims=True)
    exponent = jnp.exp(masked - top_score)
    row_total = jnp.sum(exponent, axis=-1, keepdims=True)
    return (exponent / row_total, top_score[..., 0] + jnp.log(row_total[..., 0]))


def on_device(
    hidden,
    condition,
    caption,
    lengths,
    frames,
    widths,
    caption_lens,
    cotangent,
    ada_weight,
    ada_bias,
    norm_gains,
    qkv_weight,
    head_gains,
    caption_weight,
    head_gate,
    out_weight,
    ffn_weight,
    down_weight,
):
    tensor_id = lax.axis_index("tensor")
    tensor_count = lax.axis_size("tensor")
    full_ada, full_bias, full_gains, full_qkv, full_caption, full_out, full_ffn, full_down = (
        lax.all_gather(ada_weight, "dp", axis=0, tiled=True),
        lax.all_gather(ada_bias, "dp", axis=0, tiled=True),
        lax.all_gather(norm_gains, "dp", axis=1, tiled=True),
        lax.all_gather(qkv_weight, "dp", axis=1, tiled=True),
        lax.all_gather(caption_weight, "dp", axis=1, tiled=True),
        lax.all_gather(out_weight, "dp", axis=1, tiled=True),
        lax.all_gather(ffn_weight, "dp", axis=1, tiled=True),
        lax.all_gather(down_weight, "dp", axis=1, tiled=True),
    )
    model_width = full_gains.shape[1]
    row_count = hidden.shape[2]
    seq_len = row_count * tensor_count
    text_count = caption.shape[2]
    local_cols = full_ada.shape[1]
    local_width = full_qkv.shape[2]
    local_heads = local_width // HD
    batches = hidden.shape[0]
    scaling = HD ** (-0.5)
    block_rows = min(512, seq_len)
    block_count = seq_len // block_rows
    gains_float = full_gains.astype(jnp.float32)
    head_scales = head_gains.astype(jnp.float32)
    gate_values = jnp.tanh(
        lax.dynamic_slice_in_dim(
            head_gate.astype(jnp.float32), tensor_id * local_heads, local_heads, 0
        )
    )
    unit_rows = swish(condition[:, 0].astype(jnp.float32)).astype(jnp.bfloat16)
    bias_cols = lax.dynamic_slice_in_dim(full_bias, tensor_id * local_cols, local_cols, 0).astype(
        jnp.float32
    )
    mod_cols = jnp.dot(unit_rows, full_ada, preferred_element_type=jnp.float32) + bias_cols
    modulation = lax.all_gather(mod_cols, "tensor", axis=1, tiled=True)
    slot_rows = tensor_id * row_count + jnp.arange(row_count, dtype=jnp.int32)
    head_shape = (seq_len, local_heads, HD)
    text_shape = (text_count, local_heads, HD)
    totals = None
    ffn_acc = None
    down_acc = None
    out_list = []
    grad_list = []
    for batch_index in range(batches):
        resid = hidden[batch_index, 0].astype(jnp.float32)
        length = lengths[batch_index, 0]
        live_rows = (slot_rows < length).astype(jnp.float32)[:, None]
        key_live = jnp.arange(seq_len, dtype=jnp.int32) < length
        text_live = jnp.arange(text_count, dtype=jnp.int32) < caption_lens[batch_index, 0]
        cosine, sine_table = rope_tables(
            length, frames[batch_index, 0], widths[batch_index, 0], seq_len, HD
        )
        mod_rows = modulation[batch_index].reshape(4, model_width)
        scale_attn, gate_attn, scale_ffn, gate_ffn = (
            mod_rows[0],
            mod_rows[1],
            mod_rows[2],
            mod_rows[3],
        )
        unit_one, inverse_one = normalize(resid)
        first_in = (unit_one * gains_float[0] * (1.0 + scale_attn)).astype(jnp.bfloat16)
        gathered_one = lax.all_gather(first_in, "tensor", axis=0, tiled=True)
        projected = jnp.einsum(
            "sd,cdk->csk", gathered_one, full_qkv, preferred_element_type=jnp.float32
        )
        query_unit, query_inverse = normalize(projected[0].reshape(head_shape))
        key_unit, key_inverse = normalize(projected[1].reshape(head_shape))
        queries = rotate(query_unit * head_scales[0], cosine, sine_table).astype(jnp.bfloat16)
        keys = rotate(key_unit * head_scales[1], cosine, sine_table).astype(jnp.bfloat16)
        values = projected[2].reshape(head_shape).astype(jnp.bfloat16)
        text_proj = jnp.einsum(
            "td,cdk->ctk", caption[batch_index, 0], full_caption, preferred_element_type=jnp.float32
        )
        text_unit, text_inverse = normalize(text_proj[0].reshape(text_shape))
        text_keys = (text_unit * head_scales[2]).astype(jnp.bfloat16)
        text_values = text_proj[1].reshape(text_shape).astype(jnp.bfloat16)

        def attend(query_block):
            scores = (
                jnp.einsum("qhd,khd->hqk", query_block, keys, preferred_element_type=jnp.float32)
                * scaling
            )
            probs, lse_self = softmax_parts(scores, key_live)
            own = jnp.einsum(
                "hqk,khd->qhd",
                probs.astype(jnp.bfloat16),
                values,
                preferred_element_type=jnp.float32,
            )
            text_scores = (
                jnp.einsum(
                    "qhd,khd->hqk", query_block, text_keys, preferred_element_type=jnp.float32
                )
                * scaling
            )
            text_probs, lse_text = softmax_parts(text_scores, text_live)
            other = jnp.einsum(
                "hqk,khd->qhd",
                text_probs.astype(jnp.bfloat16),
                text_values,
                preferred_element_type=jnp.float32,
            )
            return (own, other, lse_self, lse_text)

        query_blocks = queries.reshape(block_count, block_rows, local_heads, HD)
        own_all, other_all, lse_self_all, lse_text_all = lax.map(attend, query_blocks)
        other_heads = other_all.reshape(head_shape)
        combined = (
            (own_all.reshape(head_shape) + gate_values[None, :, None] * other_heads)
            .astype(jnp.bfloat16)
            .reshape(seq_len, local_width)
        )
        attn = lax.psum_scatter(
            jnp.dot(combined, full_out, preferred_element_type=jnp.float32),
            "tensor",
            scatter_dimension=0,
            tiled=True,
        )
        unit_two, inverse_two = normalize(attn)
        gate_a = jnp.tanh(gate_attn)
        middle = resid + live_rows * gate_a * unit_two * gains_float[1]
        unit_three, inverse_three = normalize(middle)
        second_in = (unit_three * gains_float[2] * (1.0 + scale_ffn)).astype(jnp.bfloat16)
        gathered_two = lax.all_gather(second_in, "tensor", axis=0, tiled=True)
        pre_act = jnp.einsum(
            "sd,cdf->csf", gathered_two, full_ffn, preferred_element_type=jnp.float32
        )
        activated = (swish(pre_act[0]) * pre_act[1]).astype(jnp.bfloat16)
        ffn_total = lax.psum_scatter(
            jnp.dot(activated, full_down, preferred_element_type=jnp.float32),
            "tensor",
            scatter_dimension=0,
            tiled=True,
        )
        unit_four, inverse_four = normalize(ffn_total)
        gate_f = jnp.tanh(gate_ffn)
        out_list.append(
            (middle + live_rows * gate_f * unit_four * gains_float[3]).astype(jnp.bfloat16)
        )
        grad_top = cotangent[batch_index, 0].astype(jnp.float32)
        weighted = grad_top * live_rows
        gain_four = jnp.sum(weighted * gate_f * unit_four, axis=0)
        gate_ffn_grad = jnp.sum(weighted * unit_four * gains_float[3], axis=0) * (
            1.0 - gate_f * gate_f
        )
        grad_ffn_in = norm_back(unit_four, inverse_four, weighted * gate_f * gains_float[3]).astype(
            jnp.bfloat16
        )
        gathered_grad_two = lax.all_gather(grad_ffn_in, "tensor", axis=0, tiled=True)
        grad_act = jnp.einsum(
            "sd,fd->sf", gathered_grad_two, full_down, preferred_element_type=jnp.float32
        )
        down_grad = jnp.einsum(
            "sf,sd->fd", activated, gathered_grad_two, preferred_element_type=jnp.float32
        )
        sigma = jax.nn.sigmoid(pre_act[0])
        grad_pre = jnp.stack(
            [
                grad_act * pre_act[1] * sigma * (1.0 + pre_act[0] * (1.0 - sigma)),
                grad_act * swish(pre_act[0]),
            ]
        ).astype(jnp.bfloat16)
        ffn_grad = jnp.einsum(
            "sd,csf->cdf", gathered_two, grad_pre, preferred_element_type=jnp.float32
        )
        if ffn_acc is None:
            ffn_acc, down_acc = (ffn_grad, down_grad)
        else:
            ffn_acc, down_acc = (ffn_acc + ffn_grad, down_acc + down_grad)
        grad_second = lax.psum_scatter(
            jnp.einsum("csf,cdf->sd", grad_pre, full_ffn, preferred_element_type=jnp.float32),
            "tensor",
            scatter_dimension=0,
            tiled=True,
        )
        scale_ffn_grad = jnp.sum(grad_second * unit_three * gains_float[2], axis=0)
        gain_three = jnp.sum(grad_second * (1.0 + scale_ffn) * unit_three, axis=0)
        grad_middle = grad_top + norm_back(
            unit_three, inverse_three, grad_second * (1.0 + scale_ffn) * gains_float[2]
        )
        weighted_mid = grad_middle * live_rows
        gain_two = jnp.sum(weighted_mid * gate_a * unit_two, axis=0)
        gate_attn_grad = jnp.sum(weighted_mid * unit_two * gains_float[1], axis=0) * (
            1.0 - gate_a * gate_a
        )
        grad_attn_in = norm_back(
            unit_two, inverse_two, weighted_mid * gate_a * gains_float[1]
        ).astype(jnp.bfloat16)
        gathered_grad_one = lax.all_gather(grad_attn_in, "tensor", axis=0, tiled=True)
        grad_combined = jnp.einsum(
            "sd,kd->sk", gathered_grad_one, full_out, preferred_element_type=jnp.float32
        ).astype(jnp.bfloat16)
        out_grad = jnp.einsum(
            "sk,sd->kd", combined, gathered_grad_one, preferred_element_type=jnp.float32
        )
        grad_heads = grad_combined.reshape(head_shape)
        gate_local = jnp.sum(grad_heads.astype(jnp.float32) * other_heads, axis=(0, 2)) * (
            1.0 - gate_values * gate_values
        )
        grad_text_heads = (gate_values[None, :, None] * grad_heads.astype(jnp.float32)).astype(
            jnp.bfloat16
        )

        def attend_back(carry, blocks):
            grad_keys, grad_values, grad_text_keys, grad_text_values = carry
            query_block, grad_block, text_grad_block, lse_block, lse_text_block = blocks
            scores = (
                jnp.einsum("qhd,khd->hqk", query_block, keys, preferred_element_type=jnp.float32)
                * scaling
            )
            scores = jnp.where(key_live[None, None, :], scores, NEGATIVE)
            probs = jnp.exp(scores - lse_block[..., None])
            grad_values = grad_values + jnp.einsum(
                "hqk,qhd->khd",
                probs.astype(jnp.bfloat16),
                grad_block,
                preferred_element_type=jnp.float32,
            )
            grad_probs = jnp.einsum(
                "qhd,khd->hqk", grad_block, values, preferred_element_type=jnp.float32
            )
            grad_scores = (
                probs * (grad_probs - jnp.sum(probs * grad_probs, axis=-1, keepdims=True))
            ).astype(jnp.bfloat16)
            grad_query = (
                jnp.einsum("hqk,khd->qhd", grad_scores, keys, preferred_element_type=jnp.float32)
                * scaling
            )
            grad_keys = (
                grad_keys
                + jnp.einsum(
                    "hqk,qhd->khd", grad_scores, query_block, preferred_element_type=jnp.float32
                )
                * scaling
            )
            text_scores = (
                jnp.einsum(
                    "qhd,khd->hqk", query_block, text_keys, preferred_element_type=jnp.float32
                )
                * scaling
            )
            text_scores = jnp.where(text_live[None, None, :], text_scores, NEGATIVE)
            text_probs = jnp.exp(text_scores - lse_text_block[..., None])
            grad_text_values = grad_text_values + jnp.einsum(
                "hqk,qhd->khd",
                text_probs.astype(jnp.bfloat16),
                text_grad_block,
                preferred_element_type=jnp.float32,
            )
            grad_text_probs = jnp.einsum(
                "qhd,khd->hqk", text_grad_block, text_values, preferred_element_type=jnp.float32
            )
            grad_text_scores = (
                text_probs
                * (grad_text_probs - jnp.sum(text_probs * grad_text_probs, axis=-1, keepdims=True))
            ).astype(jnp.bfloat16)
            grad_query = (
                grad_query
                + jnp.einsum(
                    "hqk,khd->qhd", grad_text_scores, text_keys, preferred_element_type=jnp.float32
                )
                * scaling
            )
            grad_text_keys = (
                grad_text_keys
                + jnp.einsum(
                    "hqk,qhd->khd",
                    grad_text_scores,
                    query_block,
                    preferred_element_type=jnp.float32,
                )
                * scaling
            )
            return ((grad_keys, grad_values, grad_text_keys, grad_text_values), grad_query)

        zero_heads = jnp.zeros(head_shape, jnp.float32)
        zero_text = jnp.zeros(text_shape, jnp.float32)
        block_shape = (block_count, block_rows, local_heads, HD)
        carried, grad_query_blocks = lax.scan(
            attend_back,
            (zero_heads, zero_heads, zero_text, zero_text),
            (
                query_blocks,
                grad_heads.reshape(block_shape),
                grad_text_heads.reshape(block_shape),
                lse_self_all,
                lse_text_all,
            ),
        )
        grad_keys, grad_values, grad_text_keys, grad_text_values = carried
        grad_query_rot = rotate_back(grad_query_blocks.reshape(head_shape), cosine, sine_table)
        grad_key_rot = rotate_back(grad_keys, cosine, sine_table)
        head_query = jnp.sum(grad_query_rot * query_unit, axis=(0, 1))
        head_key = jnp.sum(grad_key_rot * key_unit, axis=(0, 1))
        head_text = jnp.sum(grad_text_keys * text_unit, axis=(0, 1))
        grad_q_raw = norm_back(query_unit, query_inverse, grad_query_rot * head_scales[0]).astype(
            jnp.bfloat16
        )
        grad_k_raw = norm_back(key_unit, key_inverse, grad_key_rot * head_scales[1]).astype(
            jnp.bfloat16
        )
        grad_proj = jnp.stack(
            [
                grad_q_raw.reshape(seq_len, local_width),
                grad_k_raw.reshape(seq_len, local_width),
                grad_values.reshape(seq_len, local_width).astype(jnp.bfloat16),
            ]
        )
        grad_text_raw = norm_back(text_unit, text_inverse, grad_text_keys * head_scales[2]).astype(
            jnp.bfloat16
        )
        text_grad = jnp.stack(
            [
                grad_text_raw.reshape(text_count, local_width),
                grad_text_values.reshape(text_count, local_width).astype(jnp.bfloat16),
            ]
        )
        qkv_grad = jnp.einsum(
            "sd,csk->cdk", gathered_one, grad_proj, preferred_element_type=jnp.float32
        )
        caption_grad = jnp.einsum(
            "td,ctk->cdk", caption[batch_index, 0], text_grad, preferred_element_type=jnp.float32
        )
        grad_first = lax.psum_scatter(
            jnp.einsum(
                "csk,cdk->sd", grad_proj, full_qkv, preferred_element_type=jnp.float32
            ).astype(jnp.bfloat16),
            "tensor",
            scatter_dimension=0,
            tiled=True,
        ).astype(jnp.float32)
        scale_attn_grad = jnp.sum(grad_first * unit_one * gains_float[0], axis=0)
        gain_one = jnp.sum(grad_first * (1.0 + scale_attn) * unit_one, axis=0)
        grad_list.append(
            grad_middle
            + norm_back(unit_one, inverse_one, grad_first * (1.0 + scale_attn) * gains_float[0])
        )
        mod_grad = jnp.concatenate(
            [scale_attn_grad, gate_attn_grad, scale_ffn_grad, gate_ffn_grad]
        )[None, :]
        gain_grad = jnp.stack([gain_one, gain_two, gain_three, gain_four])
        head_grad = jnp.stack([head_query, head_key, head_text])
        gate_grad = lax.dynamic_update_slice_in_dim(
            jnp.zeros((H,), jnp.float32), gate_local, tensor_id * local_heads, 0
        )
        pieces = (mod_grad, gain_grad, head_grad, gate_grad, qkv_grad, caption_grad, out_grad)
        if totals is None:
            totals = pieces
        else:
            totals = (jnp.concatenate([totals[0], pieces[0]], axis=0),) + tuple(
                (left + right for left, right in zip(totals[1:], pieces[1:]))
            )
    mod_part, gain_part, head_part, gate_part, qkv_part, caption_part, out_part = totals
    mod_total = lax.psum(mod_part.astype(jnp.bfloat16), "tensor").astype(jnp.float32)
    gain_total = lax.psum(gain_part.astype(jnp.bfloat16), "tensor")
    head_total = lax.psum(head_part.astype(jnp.bfloat16), "tensor").astype(jnp.float32)
    gate_total = lax.psum(gate_part.astype(jnp.bfloat16), "tensor").astype(jnp.float32)
    mod_local = lax.dynamic_slice_in_dim(mod_total, tensor_id * local_cols, local_cols, 1)
    ada_grad = jnp.einsum(
        "mc,mk->ck", unit_rows.astype(jnp.float32), mod_local, precision=lax.Precision.HIGHEST
    )
    bias_grad = jnp.sum(mod_total, axis=0)
    ffn_shard = lax.psum_scatter(
        ffn_acc.astype(jnp.bfloat16), "dp", scatter_dimension=1, tiled=True
    ).astype(jnp.float32)
    down_shard = lax.psum_scatter(
        down_acc.astype(jnp.bfloat16), "dp", scatter_dimension=1, tiled=True
    ).astype(jnp.float32)
    head_done, gate_done = lax.psum((head_total, gate_total), "dp")
    layer_out = jnp.stack(out_list)[:, None]
    grad_hidden = jnp.stack(grad_list)[:, None]
    return (
        layer_out,
        grad_hidden,
        lax.psum_scatter(
            ada_grad.astype(jnp.bfloat16), "dp", scatter_dimension=0, tiled=True
        ).astype(jnp.float32),
        lax.psum_scatter(
            bias_grad.astype(jnp.bfloat16), "dp", scatter_dimension=0, tiled=True
        ).astype(jnp.float32),
        lax.psum_scatter(gain_total, "dp", scatter_dimension=1, tiled=True).astype(jnp.float32),
        lax.psum_scatter(
            qkv_part.astype(jnp.bfloat16), "dp", scatter_dimension=1, tiled=True
        ).astype(jnp.float32),
        head_done,
        lax.psum_scatter(
            caption_part.astype(jnp.bfloat16), "dp", scatter_dimension=1, tiled=True
        ).astype(jnp.float32),
        gate_done,
        lax.psum_scatter(
            out_part.astype(jnp.bfloat16), "dp", scatter_dimension=1, tiled=True
        ).astype(jnp.float32),
        ffn_shard,
        down_shard,
    )


def solution(mesh):
    return jax.shard_map(
        on_device,
        mesh=mesh,
        in_specs=(
            P(None, "dp", "tensor", None),
            P(None, "dp", None),
            P(None, "dp", None, None),
            P(None, "dp"),
            P(None, "dp"),
            P(None, "dp"),
            P(None, "dp"),
            P(None, "dp", "tensor", None),
            P("dp", "tensor"),
            P("dp"),
            P(None, "dp"),
            P(None, "dp", "tensor"),
            P(),
            P(None, "dp", "tensor"),
            P(),
            P("tensor", "dp"),
            P(None, "dp", "tensor"),
            P("tensor", "dp"),
        ),
        out_specs=(
            P(None, "dp", "tensor", None),
            P(None, "dp", "tensor", None),
            P("dp", "tensor"),
            P("dp"),
            P(None, "dp"),
            P(None, "dp", "tensor"),
            P(),
            P(None, "dp", "tensor"),
            P(),
            P("tensor", "dp"),
            P(None, "dp", "tensor"),
            P("tensor", "dp"),
        ),
        check_vma=False,
    )
```

profile of v0, /device:TPU:1, one launch (start us, length us, event | category | flops | bytes accessed | tf_op | source)
XLA Modules:
  0.0 1791.5 jit_solution(5347005757886025371)
XLA Ops:
  105.9 32.5 %all_gather.58 = bf16[192,1536]{0,1:T(8,128)(2,1)} all-gather(bf16[192,96]{0,1:T(8,128)(2,1)S(1)} %copy.146), channel_id=1, replica_groups=mesh['dp'=16,'tensor'=8] {'dp'}, dimensions={1}, use_global_device_ids=true | all-gather | bytes 626688 | tf_op jit(solution)/shard_map/all_gather | solution.py:120
  159.4 41.5 %all-gather.18.cloned.1.call-done = bf16[512,1536]{1,0:T(8,128)(2,1)} async-done(((bf16[64,1536]{1,0:T(8,128)(2,1)}), bf16[512,1536]{1,0:T(8,128)(2,1)}) %all-gather.18.cloned.1.call-update) | async-done | bytes 1572880 | tf_op jit(solution)/shard_map/all_gather | solution.py:174
  208.4 48.3 %all-gather.22.cloned.1.call-done = bf16[2,4096,192]{1,2,0:T(8,128)(2,1)} async-done(((bf16[2,256,192]{1,2,0:T(8,128)(2,1)}), bf16[2,4096,192]{1,2,0:T(8,128)(2,1)}) %all-gather.22.cloned.1.call-update) | async-done | bytes 3145744 | tf_op jit(solution)/shard_map/all_gather | solution.py:119
  283.9 54.5 %reduce-scatter.25.cloned.1.call-done = f32[64,1536]{1,0:T(8,128)} async-done(((f32[512,1536]{1,0:T(8,128)}), f32[64,1536]{1,0:T(8,128)}) %reduce-scatter.25.cloned.1.call-update) | async-done | bytes 393232 | tf_op jit(solution)/shard_map/reduce_scatter | solution.py:225
  340.1 72.3 %reduce-scatter.21.cloned.1.call-done = f32[64,1536]{1,0:T(8,128)} async-done(((f32[512,1536]{1,0:T(8,128)}), f32[64,1536]{1,0:T(8,128)}) %reduce-scatter.21.cloned.1.call-update) | async-done | bytes 393232 | tf_op jit(solution)/shard_map/reduce_scatter | solution.py:225
  418.9 46.8 %all-gather.26.cloned.1.call-done = bf16[2,1536,512]{2,1,0:T(8,128)(2,1)} async-done(((bf16[2,96,512]{2,1,0:T(8,128)(2,1)}), bf16[2,1536,512]{2,1,0:T(8,128)(2,1)}) %all-gather.26.cloned.1.call-update) | async-done | bytes 3145744 | tf_op jit(solution)/shard_map/all_gather | solution.py:121
  465.6 42.1 %all-gather.24.cloned.1.call-done = bf16[512,1536]{1,0:T(8,128)(2,1)} async-done(((bf16[64,1536]{1,0:T(8,128)(2,1)}), bf16[512,1536]{1,0:T(8,128)(2,1)}) %all-gather.24.cloned.1.call-update) | async-done | bytes 1572880 | tf_op jit(solution)/shard_map/all_gather | solution.py:236
  514.3 43.8 %all-gather.28.cloned.1.call-done = bf16[512,1536]{0,1:T(8,128)(2,1)} async-done(((bf16[512,96]{0,1:T(8,128)(2,1)}), bf16[512,1536]{0,1:T(8,128)(2,1)}) %all-gather.28.cloned.1.call-update) | async-done | bytes 1572880 | tf_op jit(solution)/shard_map/all_gather | solution.py:122
  562.6 37.7 %all-gather.32.cloned.1.call-done = bf16[512,1536]{1,0:T(8,128)(2,1)} async-done(((bf16[64,1536]{1,0:T(8,128)(2,1)}), bf16[512,1536]{1,0:T(8,128)(2,1)}) %all-gather.32.cloned.1.call-update) | async-done | bytes 1572880 | tf_op jit(solution)/shard_map/all_gather | solution.py:236
  610.2 65.8 %reduce-scatter.23.cloned.1.call-done = f32[64,1536]{1,0:T(8,128)} async-done(((f32[512,1536]{1,0:T(8,128)}), f32[64,1536]{1,0:T(8,128)}) %reduce-scatter.23.cloned.1.call-update) | async-done | bytes 393232 | tf_op jit(solution)/shard_map/reduce_scatter | solution.py:241
  677.6 72.3 %reduce-scatter.27.cloned.1.call-done = f32[64,1536]{1,0:T(8,128)} async-done(((f32[512,1536]{1,0:T(8,128)}), f32[64,1536]{1,0:T(8,128)}) %reduce-scatter.27.cloned.1.call-update) | async-done | bytes 393232 | tf_op jit(solution)/shard_map/reduce_scatter | solution.py:241
  756.7 40.6 %all-gather.34.cloned.1.call-done = bf16[512,1536]{1,0:T(8,128)(2,1)} async-done(((bf16[64,1536]{1,0:T(8,128)(2,1)}), bf16[512,1536]{1,0:T(8,128)(2,1)}) %all-gather.34.cloned.1.call-update) | async-done | bytes 1572880 | tf_op jit(solution)/shard_map/all_gather | solution.py:261
  805.8 36.5 %all-gather.38.cloned.1.call-done = bf16[512,1536]{1,0:T(8,128)(2,1)} async-done(((bf16[64,1536]{1,0:T(8,128)(2,1)}), bf16[512,1536]{1,0:T(8,128)(2,1)}) %all-gather.38.cloned.1.call-update) | async-done | bytes 1572880 | tf_op jit(solution)/shard_map/all_gather | solution.py:261
  850.8 67.1 %reduce-scatter.29.cloned.1.call-done = f32[64,1536]{1,0:T(8,128)} async-done(((f32[512,1536]{1,0:T(8,128)}), f32[64,1536]{1,0:T(8,128)}) %reduce-scatter.29.cloned.1.call-update) | async-done | bytes 393232 | tf_op jit(solution)/shard_map/reduce_scatter | solution.py:282
  920.3 71.4 %reduce-scatter.33.cloned.1.call-done = f32[64,1536]{1,0:T(8,128)} async-done(((f32[512,1536]{1,0:T(8,128)}), f32[64,1536]{1,0:T(8,128)}) %reduce-scatter.33.cloned.1.call-update) | async-done | bytes 393232 | tf_op jit(solution)/shard_map/reduce_scatter | solution.py:282
  1046.7 36.5 %all-gather.40.cloned.1.call-done = bf16[512,1536]{1,0:T(8,128)(2,1)} async-done(((bf16[64,1536]{1,0:T(8,128)(2,1)}), bf16[512,1536]{1,0:T(8,128)(2,1)}) %all-gather.40.cloned.1.call-update) | async-done | bytes 1572880 | tf_op jit(solution)/shard_map/all_gather | solution.py:301
  1148.5 45.9 %reduce-scatter.35.cloned.1.call-done = bf16[64,1536]{1,0:T(8,128)(2,1)} async-done(((bf16[512,1536]{1,0:T(8,128)(2,1)}), bf16[64,1536]{1,0:T(8,128)(2,1)}) %reduce-scatter.35.cloned.1.call-update) | async-done | bytes 196624 | tf_op jit(solution)/shard_map/reduce_scatter | solution.py:436
  1298.4 39.9 %reduce-scatter.41.cloned.1.call-done = bf16[512,96]{0,1:T(8,128)(2,1)} async-done(((bf16[512,1536]{0,1:T(8,128)(2,1)}), bf16[512,96]{0,1:T(8,128)(2,1)}) %reduce-scatter.41.cloned.1.call-update) | async-done | bytes 98320 | tf_op jit(solution)/shard_map/reduce_scatter | solution.py:478
  1339.9 148.5 %all-reduce.6.cloned.1.call-done = bf16[2,1536,512]{2,0,1:T(2,128)(2,1)} async-done(((bf16[2,1536,512]{2,0,1:T(2,128)(2,1)}), bf16[2,1536,512]{2,0,1:T(2,128)(2,1)}) %all-reduce.6.cloned.1.call-update) | async-done | bytes 3145744
  1490.2 67.4 %reduce-scatter.45.cloned.1.call-done = bf16[96,192]{1,0:T(8,128)(2,1)} async-done(((bf16[1536,192]{1,0:T(8,128)(2,1)}), bf16[96,192]{1,0:T(8,128)(2,1)}) %reduce-scatter.45.cloned.1.call-update) | async-done | bytes 36880
  1559.2 72.3 %reduce-scatter.43.cloned.1.call-done = bf16[96,576]{1,0:T(8,128)(2,1)} async-done(((bf16[1536,576]{1,0:T(8,128)(2,1)}), bf16[96,576]{1,0:T(8,128)(2,1)}) %reduce-scatter.43.cloned.1.call-update) | async-done | bytes 110608
  1635.6 36.1 %all-reduce.2 = (f32[3,64]{1,0:T(4,128)}, f32[24]{0:T(128)}) all-reduce(bf16[3,64]{1,0:T(4,128)(2,1)S(1)} %get-tuple-element.306, bf16[24]{0:T(256)(128)(2,1)S(1)} %get-tuple-element.307), channel_id=1, replica_groups=mesh['dp'=16,'tensor'=8] {'dp'}, use_global_device_ids=true, to_apply=%region_80.81 | all-reduce | flops 216 | bytes 1296 | tf_op jit(solution)/shard_map/psum | solution.py:481
  1671.7 60.1 %all-reduce = bf16[6144]{0:T(1024)(128)(2,1)S(1)} all-reduce(bf16[6144]{0:T(1024)(128)(2,1)S(1)} %reduce_sum.630), channel_id=11, replica_groups=mesh['dp'=16,'tensor'=8] {'dp'}, use_global_device_ids=true, to_apply=%region_57.58.clone | all-reduce | flops 6144 | bytes 24576
  1734.2 48.5 %reduce-scatter.37.cloned.1.call-done = bf16[64,768]{1,0:T(8,128)(2,1)} async-done(((bf16[1024,768]{1,0:T(8,128)(2,1)}), bf16[64,768]{1,0:T(8,128)(2,1)}) %reduce-scatter.37.cloned.1.call-update) | async-done | bytes 98320 | tf_op jit(solution)/shard_map/reduce_scatter | solution.py:487
  (820 shorter events, 436.2 us)
Async XLA Ops:
  7.9 130.5 %all-gather.20.cloned.1.call-start = ((), (), s32[]{:S(2)}) async-start(), calls=%async_computation.16 | async-start | bytes 3342336 | tf_op jit(solution)/shard_map/all_gather | solution.py:118
  9.7 145.9 %all-gather.30.cloned.1.call-start = ((), (), s32[]{:S(2)}) async-start(), calls=%async_computation.23 | async-start | bytes 1769472 | tf_op jit(solution)/shard_map/all_gather | solution.py:174
  86.1 114.8 %all-gather.18.cloned.1.call-start = ((), (), s32[]{:S(2)}) async-start(), calls=%async_computation.15 | async-start | bytes 1769472 | tf_op jit(solution)/shard_map/all_gather | solution.py:174
  86.7 170.0 %all-gather.22.cloned.1.call-start = ((), (), s32[]{:S(2)}) async-start(), calls=%async_computation.17 | async-start | bytes 3342336 | tf_op jit(solution)/shard_map/all_gather | solution.py:119
  87.3 251.2 %reduce-scatter.25.cloned.1.call-start = ((), (), s32[]{:S(2)}) async-start(), calls=%async_computation.24 | async-start | bytes 3538944 | tf_op jit(solution)/shard_map/reduce_scatter | solution.py:225
  269.0 143.4 %reduce-scatter.21.cloned.1.call-start = ((), (), s32[]{:S(2)}) async-start(), calls=%async_computation.18 | async-start | bytes 3538944 | tf_op jit(solution)/shard_map/reduce_scatter | solution.py:225
  281.3 184.4 %all-gather.26.cloned.1.call-start = ((), (), s32[]{:S(2)}) async-start(), calls=%async_computation.20 | async-start | bytes 3342336 | tf_op jit(solution)/shard_map/all_gather | solution.py:121
  282.0 225.7 %all-gather.24.cloned.1.call-start = ((), (), s32[]{:S(2)}) async-start(), calls=%async_computation.19 | async-start | bytes 1769472 | tf_op jit(solution)/shard_map/all_gather | solution.py:236
  417.5 140.7 %all-gather.28.cloned.1.call-start = ((), (), s32[]{:S(2)}) async-start(), calls=%async_computation.21 | async-start | bytes 1671168 | tf_op jit(solution)/shard_map/all_gather | solution.py:122
  418.1 182.1 %all-gather.32.cloned.1.call-start = ((), (), s32[]{:S(2)}) async-start(), calls=%async_computation.25 | async-start | bytes 1769472 | tf_op jit(solution)/shard_map/all_gather | solution.py:236
  418.8 257.1 %reduce-scatter.23.cloned.1.call-start = ((), (), s32[]{:S(2)}) async-start(), calls=%async_computation.22 | async-start | bytes 3538944 | tf_op jit(solution)/shard_map/reduce_scatter | solution.py:241
  562.5 187.4 %reduce-scatter.27.cloned.1.call-start = ((), (), s32[]{:S(2)}) async-start(), calls=%async_computation.26 | async-start | bytes 3538944 | tf_op jit(solution)/shard_map/reduce_scatter | solution.py:241
  610.1 187.1 %all-gather.34.cloned.1.call-start = ((), (), s32[]{:S(2)}) async-start(), calls=%async_computation.27 | async-start | bytes 1769472 | tf_op jit(solution)/shard_map/all_gather | solution.py:261
  756.6 161.3 %reduce-scatter.29.cloned.1.call-start = ((), (), s32[]{:S(2)}) async-start(), calls=%async_computation.28 | async-start | bytes 3538944 | tf_op jit(solution)/shard_map/reduce_scatter | solution.py:282
  805.7 186.0 %reduce-scatter.33.cloned.1.call-start = ((), (), s32[]{:S(2)}) async-start(), calls=%async_computation.32 | async-start | bytes 3538944 | tf_op jit(solution)/shard_map/reduce_scatter | solution.py:282
  850.7 187.3 %all-gather.36.cloned.1.call-start = ((), (), s32[]{:S(2)}) async-start(), calls=%async_computation.29 | async-start | bytes 1769472 | tf_op jit(solution)/shard_map/all_gather | solution.py:301
  999.5 149.0 %reduce-scatter.31.cloned.1.call-start = ((), (), s32[]{:S(2)}) async-start(), calls=%async_computation.30 | async-start | bytes 1769472 | tf_op jit(solution)/shard_map/reduce_scatter | solution.py:436
  1114.3 151.7 %reduce-scatter.47.cloned.1.call-start = ((), (), s32[]{:S(2)}) async-start(), calls=%async_computation.40 | async-start | bytes 417792
  1199.7 138.5 %reduce-scatter.41.cloned.1.call-start = ((), (), s32[]{:S(2)}) async-start(), calls=%async_computation.37 | async-start | bytes 1671168 | tf_op jit(solution)/shard_map/reduce_scatter | solution.py:478
  1203.6 284.8 %all-reduce.6.cloned.1.call-start = ((), (), s32[]{:S(2)}) async-start(), calls=%async_computation.41 | async-start | bytes 6291456
  1216.1 341.6 %reduce-scatter.45.cloned.1.call-start = ((), (), s32[]{:S(2)}) async-start(), calls=%async_computation.39 | async-start | bytes 835584
  1220.7 410.8 %reduce-scatter.43.cloned.1.call-start = ((), (), s32[]{:S(2)}) async-start(), calls=%async_computation.38 | async-start | bytes 2088960
  1233.9 498.6 %reduce-scatter.39.cloned.1.call-start = ((), (), s32[]{:S(2)}) async-start(), calls=%async_computation.36 | async-start | bytes 3342336 | tf_op jit(solution)/shard_map/reduce_scatter | solution.py:498
  1244.1 538.5 %reduce-scatter.37.cloned.1.call-start = ((), (), s32[]{:S(2)}) async-start(), calls=%async_computation.35 | async-start | bytes 1671168 | tf_op jit(solution)/shard_map/reduce_scatter | solution.py:487
  (266 other events, 5330.8 us)
Sparse Core Ops, SparseCore 0:
  10.5 49.7 all-gather.15
  63.4 49.5 all-gather.19
  157.7 43.1 all-gather.17
  203.0 53.6 all-gather.21
  269.1 69.2 reduce-scatter.24
  340.8 71.5 reduce-scatter.20
  414.9 50.6 all-gather.25
  510.1 48.0 all-gather.27
  602.5 73.3 reduce-scatter.22
  678.3 71.5 reduce-scatter.26
  756.1 41.0 all-gather.33
  799.3 42.8 all-gather.37
  844.5 73.3 reduce-scatter.28
  920.2 71.5 reduce-scatter.32
  1040.2 42.8 all-gather.39
  1106.1 42.3 reduce-scatter.30
  1151.0 43.4 reduce-scatter.34
  1199.8 66.0 reduce-scatter.46
  1270.4 67.8 reduce-scatter.40
  1340.6 147.6 all-reduce.5
  1492.2 65.4 reduce-scatter.44
  1562.0 69.4 reduce-scatter.42
  1636.0 75.1 reduce-scatter.38
  1715.6 67.0 reduce-scatter.36
  (4 shorter events, 160.8 us)
where the time goes:
time: 1800 us; the launch traced here: 1790 us
  waiting for transfers between devices  1280 us (71%)
  blocking collectives  223 us (12%)
  matrix products  98.6 us (5%)
  other arithmetic  81.3 us (5%)
  local copies, waits for them, and re-layouts  67.6 us (4%)
  between operations  27.1 us (2%)
    unnamed x32, waiting for transfers between devices  306 us
    reduce_scatter x2, waiting for transfers between devices, on_device(): lax.psum_scatter(jnp.einsum('csf,cdf->sd', grad_pre, full_ffn, preferred_...  139 us
    reduce_scatter x2, waiting for transfers between devices, on_device(): lax.psum_scatter(jnp.dot(activated, full_down, preferred_element_type=jnp...  138 us
    reduce_scatter x2, waiting for transfers between devices, on_device(): lax.psum_scatter(jnp.dot(combined, full_out, preferred_element_type=jnp.f...  127 us
    all_gather x2, waiting for transfers between devices, on_device(): gathered_two = lax.all_gather(second_in, 'tensor', axis=0, tiled=True)  79.7 us
    all_gather x2, waiting for transfers between devices, on_device(): lax.all_gather(grad_ffn_in, 'tensor', axis=0, tiled=True)  77.1 us
    reduce_scatter x2, waiting for transfers between devices, on_device(): lax.psum_scatter(jnp.einsum('csk,cdk->sd', grad_proj, full_qkv, preferred...  73.1 us
    unnamed x1, blocking collectives  60.1 us
  transfers between devices with their start and end apart: 28, of which 26 were waited for; matrix products, arithmetic and copies ran while one was open for 10% of the time, Pallas kernels for 0%

commit v1 on v0

v1 whole, which is shorter than its diff:
```python
import functools

import jax
import jax.numpy as jnp
from jax import lax
from jax.experimental import pallas as pl
from jax.experimental.pallas import tpu as pltpu
from jax.sharding import PartitionSpec as P

D = 1536
H = 24
HD = 64
EPSILON = 1e-05
NEGATIVE = -1e30
MESH = pl.DeviceIdType.MESH
VMEM = pltpu.VMEM
F32 = jnp.float32
BF16 = jnp.bfloat16


def coords():
    dp = lax.axis_index("dp")
    t = lax.axis_index("tensor")
    return dp // 8, t % 2, (dp // 2) % 4, t // 2, dp % 2


def device_of(x, y, z, c):
    return ((x // 2) * 8 + y * 2 + c, z * 2 + x % 2)


def greet(devices):
    barrier = pltpu.get_barrier_semaphore()
    for device in devices:
        pl.semaphore_signal(barrier, inc=1, device_id=device, device_id_type=MESH)
    pl.semaphore_wait(barrier, len(devices))


class Sender:
    def __init__(self, send_sem, recv_sem):
        self.send_sem = send_sem
        self.recv_sem = recv_sem
        self.copies = []

    def __call__(self, src, dst, device):
        k = len(self.copies)
        copy = pltpu.make_async_remote_copy(
            src_ref=src,
            dst_ref=dst,
            send_sem=self.send_sem.at[k],
            recv_sem=self.recv_sem.at[k],
            device_id=device,
            device_id_type=MESH,
        )
        copy.start()
        self.copies.append(copy)
        return copy

    def drain(self):
        for copy in self.copies:
            copy.wait_send()


def dma_sems(n):
    return [pltpu.SemaphoreType.DMA((n,)), pltpu.SemaphoreType.DMA((n,))]


def kernel_call(body, inputs, out_shape, cid, scratch, in_space=VMEM, out_space=VMEM, name=None):
    single = not isinstance(out_shape, (tuple, list))
    spec = pl.BlockSpec(memory_space=out_space)
    return pl.pallas_call(
        body,
        out_shape=out_shape,
        in_specs=[pl.BlockSpec(memory_space=in_space)] * len(inputs),
        out_specs=spec if single else [spec] * len(out_shape),
        scratch_shapes=scratch,
        compiler_params=pltpu.CompilerParams(
            collective_id=cid, has_side_effects=True, vmem_limit_bytes=56 * 2**20
        ),
        name=name,
    )(*inputs)


def mod_kernel(msg_ref, ada_ref, bias_ref, got1, got3, sent, got2, s1, r1, s2, r2, s3, r3):
    dp = lax.axis_index("dp")
    t = lax.axis_index("tensor")
    dp_peers = [((dp + k) % 16, t) for k in range(1, 16)]
    t_peers = [(dp, (t + k) % 8) for k in range(1, 8)]
    greet(dp_peers + t_peers)
    first = Sender(s1, r1)
    for peer in dp_peers:
        first(msg_ref.at[peer[0]], got1.at[dp], peer)
    got1[dp] = msg_ref[dp]
    for copy in first.copies:
        copy.wait_recv()
    rows = got1[...].reshape(128, 128).astype(BF16)
    part = jnp.dot(rows, ada_ref[...], preferred_element_type=F32) + bias_ref[...]
    sent[...] = part.reshape(16, 8, 768)
    second = Sender(s2, r2)
    for peer in dp_peers:
        second(sent.at[peer[0]], got2.at[dp], peer)
    got2[dp] = sent[dp]
    for copy in second.copies:
        copy.wait_recv()
    got3[t] = jnp.sum(got2[...], axis=0)
    third = Sender(s3, r3)
    for peer in t_peers:
        third(got3.at[t], got3.at[t], peer)
    for copy in third.copies:
        copy.wait_recv()
    for sender in (first, second, third):
        sender.drain()


def hidden_kernel(hid_ref, cot_ref, all_ref, cot_out, ss, rs):
    xh, xl, y, z, c = coords()
    pair = device_of(2 * xh + 1 - xl, y, z, c)
    right = device_of(2 * xh + xl, y, (z + 1) % 4, c)
    left = device_of(2 * xh + xl, y, (z + 3) % 4, c)
    greet([pair, right, left])
    send = Sender(ss, rs)
    swap = send(hid_ref.at[1 - xl], all_ref.at[z, xl], pair)
    all_ref[z, xl] = hid_ref[xl]
    cot_swap = send(cot_ref.at[1 - xl], cot_out.at[xl], pair)
    cot_out[xl] = cot_ref[xl]
    swap.wait_recv()
    zl = (z + 3) % 4
    zr = (z + 1) % 4
    to_right = send(all_ref.at[z], all_ref.at[z], right)
    to_left = send(all_ref.at[z], all_ref.at[z], left)
    to_right.wait_recv()
    on_right = send(all_ref.at[zl, 0], all_ref.at[zl, 0], right)
    to_left.wait_recv()
    on_left = send(all_ref.at[zr, 1], all_ref.at[zr, 1], left)
    on_right.wait_recv()
    on_left.wait_recv()
    cot_swap.wait_recv()
    send.drain()


def swap_kernel(out_ref, grad_ref, out_got, grad_got, ss, rs):
    xh, xl, y, z, c = coords()
    pair = device_of(2 * xh + 1 - xl, y, z, c)
    greet([pair])
    send = Sender(ss, rs)
    a = send(out_ref.at[1 - xl], out_got.at[xl], pair)
    b = send(grad_ref.at[1 - xl], grad_got.at[xl], pair)
    a.wait_recv()
    b.wait_recv()
    send.drain()


def z_gather_kernel(x_ref, all_ref, ss, rs):
    xh, xl, y, z, c = coords()
    right = device_of(2 * xh + xl, y, (z + 1) % 4, c)
    left = device_of(2 * xh + xl, y, (z + 3) % 4, c)
    greet([left, right])
    send = Sender(ss, rs)
    to_right = send(x_ref, all_ref.at[z], right)
    to_left = send(x_ref, all_ref.at[z], left)
    all_ref[z] = x_ref[...]
    zl = (z + 3) % 4
    zr = (z + 1) % 4
    lower, upper = pl.ds(0, 64), pl.ds(64, 64)
    to_right.wait_recv()
    on_right = send(all_ref.at[zl, lower], all_ref.at[zl, lower], right)
    to_left.wait_recv()
    on_left = send(all_ref.at[zr, upper], all_ref.at[zr, upper], left)
    on_right.wait_recv()
    on_left.wait_recv()
    send.drain()


def z_scatter_kernel(x_ref, sum_ref, relay_r, relay_l, sum_r, sum_l, got_r, got_l, ss, rs):
    xh, xl, y, z, c = coords()
    right = device_of(2 * xh + xl, y, (z + 1) % 4, c)
    left = device_of(2 * xh + xl, y, (z + 3) % 4, c)
    greet([left, right])
    send = Sender(ss, rs)
    zl = (z + 3) % 4
    zr = (z + 1) % 4
    zo = (z + 2) % 4
    lower, upper = pl.ds(0, 64), pl.ds(64, 64)
    relay1 = send(x_ref.at[zo, lower], relay_r, right)
    relay2 = send(x_ref.at[zo, upper], relay_l, left)
    near1 = send(x_ref.at[zr, upper], got_r.at[upper], right)
    near2 = send(x_ref.at[zl, lower], got_l.at[lower], left)
    relay1.wait_recv()
    sum_r[...] = (relay_r[...].astype(F32) + x_ref[zr, lower].astype(F32)).astype(BF16)
    far1 = send(sum_r, got_r.at[lower], right)
    relay2.wait_recv()
    sum_l[...] = (relay_l[...].astype(F32) + x_ref[zl, upper].astype(F32)).astype(BF16)
    far2 = send(sum_l, got_l.at[upper], left)
    for copy in (near1, near2, far1, far2):
        copy.wait_recv()
    sum_ref[...] = x_ref[z].astype(F32) + got_r[...].astype(F32) + got_l[...].astype(F32)
    send.drain()


def z_gather(x, cid):
    return kernel_call(
        z_gather_kernel,
        [x],
        jax.ShapeDtypeStruct((4, 128, D), BF16),
        cid,
        dma_sems(4),
        name="z_gather%d" % cid,
    ).reshape(512, D)


def z_scatter(x, cid):
    half = VMEM((64, D), BF16)
    full = VMEM((128, D), BF16)
    return kernel_call(
        z_scatter_kernel,
        [x.reshape(4, 128, D)],
        jax.ShapeDtypeStruct((128, D), F32),
        cid,
        [half, half, half, half, full, full] + dma_sems(6),
        name="z_scatter%d" % cid,
    )


def plane_peers():
    xh, xl, y, z, c = coords()
    x = 2 * xh + xl
    xr, xq = (x + 1) % 4, (x + 3) % 4
    yr, yq = (y + 1) % 4, (y + 3) % 4
    peers = [
        device_of(xr, y, z, c),
        device_of(xq, y, z, c),
        device_of(x, yr, z, c),
        device_of(x, yq, z, c),
        device_of(x, y, z, 1 - c),
    ]
    return x, y, c, xr, xq, yr, yq, peers


def plane_gather_kernel(rows, cols, w_ref, all_ref, ss, rs, local_sem):
    x, y, c, xr, xq, yr, yq, peers = plane_peers()
    go_xr, go_xq, go_yr, go_yq, sibling = peers
    greet(peers)
    send = Sender(ss, rs)
    half = rows // 2
    top, low = pl.ds(0, half), pl.ds(half, half)

    def at(xx, yy, *rest):
        return all_ref.at[(xx % 2, xx // 2, yy, c) + rest]

    def same(ref, device):
        return send(ref, ref, device)

    local = pltpu.make_async_copy(w_ref, at(x, y), local_sem)
    local.start()
    a_r = send(w_ref.at[top], at(x, y, top), go_xr)
    a_l = send(w_ref.at[top], at(x, y, top), go_xq)
    b_r = send(w_ref.at[low], at(x, y, low), go_yr)
    b_l = send(w_ref.at[low], at(x, y, low), go_yq)
    own = send(w_ref, at(x, y), sibling)
    if rows == 96:
        left_half, right_half = pl.ds(0, cols // 2), pl.ds(cols // 2, cols // 2)
        qa = [(top, left_half), (top, right_half)]
        qb = [(low, left_half), (low, right_half)]
    else:
        q = half // 2
        qa = [(pl.ds(0, q),), (pl.ds(q, q),)]
        qb = [(pl.ds(2 * q, q),), (pl.ds(3 * q, q),)]
    a_r.wait_recv()
    f1 = same(at(xq, y, *qa[0]), go_xr)
    a_l.wait_recv()
    f2 = same(at(xr, y, *qa[1]), go_xq)
    b_r.wait_recv()
    f3 = same(at(x, yq, *qb[0]), go_yr)
    b_l.wait_recv()
    f4 = same(at(x, yr, *qb[1]), go_yq)
    for copy in (f1, f2, f3, f4):
        copy.wait_recv()
    local.wait()
    every = slice(None)
    block = all_ref.at[:, :, y, c, top]
    g_r = same(block, go_yr)
    g_l = same(block, go_yq)
    block = all_ref.at[x % 2, x // 2, :, c, low]
    h_r = same(block, go_xr)
    h_l = same(block, go_xq)
    g_r.wait_recv()
    f1 = same(all_ref.at[0, :, yq, c, top], go_yr)
    g_l.wait_recv()
    f2 = same(all_ref.at[1, :, yr, c, top], go_yq)
    h_r.wait_recv()
    f3 = same(all_ref.at[xq % 2, xq // 2, pl.ds(0, 2), c, low], go_xr)
    h_l.wait_recv()
    f4 = same(all_ref.at[xr % 2, xr // 2, pl.ds(2, 2), c, low], go_xq)
    for copy in (f1, f2, f3, f4):
        copy.wait_recv()
    late = []
    for k in range(1, 4):
        xx = (x + k) % 4
        late.append(same(all_ref.at[xx % 2, xx // 2, :, c], sibling))
    for k in range(1, 4):
        late.append(same(at(x, (y + k) % 4), sibling))
    for copy in late:
        copy.wait_recv()
    own.wait_recv()
    send.drain()


def plane_gather(w, cid):
    rows, cols = w.shape
    return kernel_call(
        functools.partial(plane_gather_kernel, rows, cols),
        [w],
        jax.ShapeDtypeStruct((2, 2, 4, 2, rows, cols), BF16),
        cid,
        dma_sems(24) + [pltpu.SemaphoreType.DMA],
        pl.ANY,
        pl.ANY,
        name="plane_gather%d" % cid,
    ).reshape(2, 16 * rows, cols)


def add_low(a, b):
    return (a.astype(F32) + b.astype(F32)).astype(BF16)


def plane_scatter_kernel(rows, cols, g_ref, out_ref, sib, ra, rb, ga, gb, pa, pb, qa, qb, ss, rs):
    x, y, c, xr, xq, yr, yq, peers = plane_peers()
    go_xr, go_xq, go_yr, go_yq, sibling = peers
    greet(peers)
    send = Sender(ss, rs)
    half = rows // 2
    top, low = pl.ds(0, half), pl.ds(half, half)
    xo, yo = (x + 2) % 4, (y + 2) % 4
    parts = []
    for k in range(4):
        parts.append(
            send(g_ref.at[k % 2, k // 2, :, 1 - c], sib.at[k % 2, k // 2], sibling)
        )
    for k in range(4):
        parts[k].wait_recv()

        def add_sibling(j, carry, k=k):
            sib[k % 2, k // 2, j] = add_low(sib[k % 2, k // 2, j], g_ref[k % 2, k // 2, j, c])
            return carry

        lax.fori_loop(0, 4, add_sibling, 0)
    t1 = send(sib.at[0, :, yo, top], ra.at[0], go_yr)
    t2 = send(sib.at[1, :, yo, top], ra.at[1], go_yq)
    l1 = send(sib.at[xo % 2, xo // 2, pl.ds(0, 2), low], rb.at[0], go_xr)
    l2 = send(sib.at[xo % 2, xo // 2, pl.ds(2, 2), low], rb.at[1], go_xq)
    t1.wait_recv()
    for j in range(2):
        sib[0, j, yr, top] = add_low(sib[0, j, yr, top], ra[0, j])
    t2.wait_recv()
    for j in range(2):
        sib[1, j, yq, top] = add_low(sib[1, j, yq, top], ra[1, j])
    t3 = send(sib.at[:, :, yr, top], ga.at[0], go_yr)
    t4 = send(sib.at[:, :, yq, top], ga.at[1], go_yq)
    l1.wait_recv()
    for j in range(2):
        sib[xr % 2, xr // 2, j, low] = add_low(sib[xr % 2, xr // 2, j, low], rb[0, j])
    l2.wait_recv()
    for j in range(2):
        sib[xq % 2, xq // 2, 2 + j, low] = add_low(sib[xq % 2, xq // 2, 2 + j, low], rb[1, j])
    l3 = send(sib.at[xr % 2, xr // 2, :, low], gb.at[0], go_xr)
    l4 = send(sib.at[xq % 2, xq // 2, :, low], gb.at[1], go_xq)
    t3.wait_recv()
    t4.wait_recv()
    for i in range(2):
        for j in range(2):
            total = (
                sib[i, j, y, top].astype(F32) + ga[0, i, j].astype(F32) + ga[1, i, j].astype(F32)
            )
            pa[i, j] = total.astype(BF16)
    q = half // 2
    q0, q1 = pl.ds(0, q), pl.ds(q, q)
    if rows == 96:
        q0 = (slice(None), pl.ds(0, cols // 2))
        q1 = (slice(None), pl.ds(cols // 2, cols // 2))
        shape0 = (half, cols // 2)
    else:
        q0, q1 = (pl.ds(0, q),), (pl.ds(q, q),)
        shape0 = (q, cols)
    e1 = send(pa.at[(xo % 2, xo // 2) + q0], qa.at[0], go_xr)
    e2 = send(pa.at[(xo % 2, xo // 2) + q1], qa.at[1], go_xq)
    l3.wait_recv()
    l4.wait_recv()
    for j in range(4):
        total = (
            sib[x % 2, x // 2, j, low].astype(F32) + gb[0, j].astype(F32) + gb[1, j].astype(F32)
        )
        pb[j] = total.astype(BF16)
    m1 = send(pb.at[(yo,) + q0], qb.at[0], go_yr)
    m2 = send(pb.at[(yo,) + q1], qb.at[1], go_yq)
    e1.wait_recv()
    ir = (xr % 2, xr // 2)
    iq = (xq % 2, xq // 2)
    pa[ir + q0] = add_low(pa[ir + q0], qa[0])
    e2.wait_recv()
    pa[iq + q1] = add_low(pa[iq + q1], qa[1])
    e3 = send(pa.at[ir], ga.at[0, 0, 0], go_xr)
    e4 = send(pa.at[iq], ga.at[1, 0, 0], go_xq)
    m1.wait_recv()
    pb[(yr,) + q0] = add_low(pb[(yr,) + q0], qb[0])
    m2.wait_recv()
    pb[(yq,) + q1] = add_low(pb[(yq,) + q1], qb[1])
    m3 = send(pb.at[yr], gb.at[0, 0], go_yr)
    m4 = send(pb.at[yq], gb.at[1, 0], go_yq)
    e3.wait_recv()
    e4.wait_recv()
    out_ref[top] = (
        pa[x % 2, x // 2].astype(F32) + ga[0, 0, 0].astype(F32) + ga[1, 0, 0].astype(F32)
    )
    m3.wait_recv()
    m4.wait_recv()
    out_ref[low] = pb[y].astype(F32) + gb[0, 0].astype(F32) + gb[1, 0].astype(F32)
    send.drain()


def plane_scatter(g, cid):
    _, total_rows, cols = g.shape
    rows = total_rows // 16
    half = rows // 2
    quarter = (half, cols // 2) if rows == 96 else (half // 2, cols)
    return kernel_call(
        functools.partial(plane_scatter_kernel, rows, cols),
        [g.reshape(2, 2, 4, 2, rows, cols)],
        jax.ShapeDtypeStruct((rows, cols), F32),
        cid,
        [
            VMEM((2, 2, 4, rows, cols), BF16),
            VMEM((2, 2, half, cols), BF16),
            VMEM((2, 2, half, cols), BF16),
            VMEM((2, 2, 2, half, cols), BF16),
            VMEM((2, 4, half, cols), BF16),
            VMEM((2, 2, half, cols), BF16),
            VMEM((4, half, cols), BF16),
            VMEM((2,) + quarter, BF16),
            VMEM((2,) + quarter, BF16),
        ]
        + dma_sems(20),
        name="plane_scatter%d" % cid,
    )


def small_kernel(mod_ref, gain_ref, g_all, gain_out, bias_all, gt, gg, gsum, s1, r1, s2, r2, s3, r3, s4, r4, s5, r5):
    dp = lax.axis_index("dp")
    t = lax.axis_index("tensor")
    dp_peers = [((dp + k) % 16, t) for k in range(1, 16)]
    t_peers = [(dp, (t + k) % 8) for k in range(1, 8)]
    greet(dp_peers + t_peers)
    first = Sender(s1, r1)
    for peer in t_peers:
        first(mod_ref.at[peer[1]], gt.at[t], peer)
    gains = Sender(s2, r2)
    for peer in dp_peers:
        gains(gain_ref.at[peer[0]], gg.at[dp], peer)
    gt[t] = mod_ref[t]
    gg[dp] = gain_ref[dp]
    for copy in first.copies:
        copy.wait_recv()
    g_all[dp, 0] = gt[0] + gt[2] + gt[4] + gt[6]
    g_all[dp, 1] = gt[1] + gt[3] + gt[5] + gt[7]
    second = Sender(s3, r3)
    for peer in dp_peers:
        second(g_all.at[dp], g_all.at[dp], peer)
    for copy in gains.copies:
        copy.wait_recv()
    gsum[t] = jnp.sum(gg[...], axis=0)
    third = Sender(s4, r4)
    for peer in t_peers:
        third(gsum.at[t], gsum.at[t], peer)
    for copy in second.copies:
        copy.wait_recv()
    bias_all[t] = jnp.sum(g_all[...], axis=(0, 1))
    fourth = Sender(s5, r5)
    for peer in t_peers:
        fourth(bias_all.at[t], bias_all.at[t], peer)
    for copy in third.copies:
        copy.wait_recv()
    gain_out[...] = jnp.sum(gsum[...], axis=0)
    for copy in fourth.copies:
        copy.wait_recv()
    for sender in (first, gains, second, third, fourth):
        sender.drain()


def normalize(values):
    inverse = lax.rsqrt(jnp.mean(values * values, axis=-1, keepdims=True) + EPSILON)
    return (values * inverse, inverse)


def norm_back(unit_values, inverse, gradient):
    return inverse * (
        gradient - unit_values * jnp.mean(gradient * unit_values, axis=-1, keepdims=True)
    )


def swish(values):
    return values * jax.nn.sigmoid(values)


def rope_tables(length, frames, width, total, head_size):
    position = jnp.arange(total, dtype=jnp.int32)
    per_frame = (length + frames - 1) // frames
    frame_pos = position // per_frame
    within = position - frame_pos * per_frame
    row_pos = within // width
    col_pos = within - row_pos * width
    half_size = head_size // 2
    time_pairs = head_size // 8
    space_pairs = (half_size - time_pairs) // 2
    pair = jnp.arange(half_size, dtype=jnp.int32)
    in_row = pair >= time_pairs
    in_col = pair >= time_pairs + space_pairs
    offset = jnp.where(in_col, time_pairs + space_pairs, jnp.where(in_row, time_pairs, 0))
    group_size = jnp.where(in_row, space_pairs, time_pairs)
    freq = 10000.0 ** (-(pair - offset).astype(jnp.float32) / group_size.astype(jnp.float32))
    chosen = jnp.where(
        in_col[None, :],
        col_pos[:, None],
        jnp.where(in_row[None, :], row_pos[:, None], frame_pos[:, None]),
    )
    angle = chosen.astype(jnp.float32) * freq[None, :]
    return (jnp.cos(angle), jnp.sin(angle))


def rotate(values, cosine, sine_table):
    half_size = values.shape[-1] // 2
    first_half = values[..., :half_size]
    second_half = values[..., half_size:]
    cos_rows = cosine[:, None, :]
    sin_rows = sine_table[:, None, :]
    return jnp.concatenate(
        [
            first_half * cos_rows - second_half * sin_rows,
            first_half * sin_rows + second_half * cos_rows,
        ],
        axis=-1,
    )


def rotate_back(gradient, cosine, sine_table):
    return rotate(gradient, cosine, -sine_table)


def pick(array, index):
    return lax.dynamic_index_in_dim(array, index, 0, keepdims=False)


def dot(spec, a, b):
    return jnp.einsum(spec, a, b, preferred_element_type=F32)


def on_device(
    hidden,
    condition,
    caption,
    lengths,
    frames,
    widths,
    caption_lens,
    cotangent,
    ada_weight,
    ada_bias,
    norm_gains,
    qkv_weight,
    head_gains,
    caption_weight,
    head_gate,
    out_weight,
    ffn_weight,
    down_weight,
):
    S = jax.ShapeDtypeStruct
    dp = lax.axis_index("dp")
    t = lax.axis_index("tensor")
    z = t // 2
    xl = t % 2
    scaling = HD ** (-0.5)
    d_shard = jnp.concatenate(
        [
            qkv_weight[0],
            qkv_weight[1],
            qkv_weight[2],
            out_weight.T,
            ffn_weight[0],
            ffn_weight[1],
            down_weight.T,
        ],
        axis=1,
    )
    c_shard = jnp.concatenate([caption_weight[0], caption_weight[1]], axis=1)
    unit_rows = swish(condition[:, 0].astype(F32)).astype(BF16)
    unit_msg = jnp.transpose(unit_rows.astype(F32).reshape(2, 16, 64), (1, 0, 2))
    unit_msg = jnp.pad(unit_msg, ((0, 0), (0, 2), (0, 64)))
    gain_msg = jnp.broadcast_to(jnp.pad(norm_gains.astype(F32), ((0, 0), (0, 32)))[None], (16, 4, 128))
    msg = jnp.concatenate([unit_msg, gain_msg], axis=1)
    ada_pad = jnp.pad(ada_weight, ((0, 64), (0, 0)))
    bias_f = ada_bias.astype(F32)
    bias_row = jnp.where(
        t == dp // 2,
        jnp.where(
            dp % 2 == 0,
            jnp.concatenate([bias_f, jnp.zeros((384,), F32)]),
            jnp.concatenate([jnp.zeros((384,), F32), bias_f]),
        ),
        0.0,
    )[None]
    got1, got3 = kernel_call(
        mod_kernel,
        [msg, ada_pad, bias_row],
        [S((16, 8, 128), F32), S((8, 8, 768), F32)],
        1,
        [VMEM((16, 8, 768), F32), VMEM((16, 8, 768), F32)]
        + dma_sems(15)
        + dma_sems(15)
        + dma_sems(7),
        name="modulation",
    )
    units = got1[:, 0:2, :64].reshape(32, 64)
    gains = jnp.transpose(got1[:, 4:8, :96], (1, 0, 2)).reshape(4, D)
    mod_rows = jnp.where(xl == 0, got3[:, 0], got3[:, 1]).reshape(4, D)
    scale_attn, gate_attn, scale_ffn, gate_ffn = (mod_rows[i] for i in range(4))
    hid_all, cot = kernel_call(
        hidden_kernel,
        [hidden[:, 0], cotangent[:, 0]],
        [S((4, 2, 64, D), BF16), S((2, 64, D), BF16)],
        2,
        dma_sems(6),
        name="hidden_gather",
    )
    resid = pick(hid_all, z).reshape(128, D).astype(F32)
    grad_top = cot.reshape(128, D).astype(F32)
    w_d = plane_gather(d_shard, 3)
    w_c = plane_gather(c_shard, 4)

    length = pick(lengths[:, 0], xl)
    frame_count = pick(frames[:, 0], xl)
    width = pick(widths[:, 0], xl)
    text_len = pick(caption_lens[:, 0], xl)
    cap = pick(caption[:, 0], xl)
    slot_rows = z * 128 + jnp.arange(128, dtype=jnp.int32)
    live_rows = (slot_rows < length).astype(F32)[:, None]
    key_live = jnp.arange(512, dtype=jnp.int32) < length
    text_live = jnp.arange(256, dtype=jnp.int32) < text_len
    cosine, sine_table = rope_tables(length, frame_count, width, 512, HD)
    head_scales = head_gains.astype(F32)
    gate_values = jnp.tanh(lax.dynamic_slice_in_dim(head_gate.astype(F32), z * 6, 6, 0))

    unit_all, _ = normalize(hid_all.reshape(512, D).astype(F32))
    first_all = (unit_all * gains[0] * (1.0 + scale_attn)).astype(BF16)
    unit_one, inverse_one = normalize(resid)
    w_q, w_k, w_v, w_o = (w_d[:, :, i * 192 : (i + 1) * 192] for i in range(4))
    w_g, w_u, w_dn = (w_d[:, :, 768 + i * 512 : 768 + (i + 1) * 512] for i in range(3))
    w_ck, w_cv = w_c[:, :, :192], w_c[:, :, 192:]
    hs = (512, 6, HD)
    ts = (256, 6, HD)
    q_raw, k_raw, v_raw = (dot("sd,xdk->sxk", first_all, w).reshape(hs) for w in (w_q, w_k, w_v))
    query_unit, query_inverse = normalize(q_raw)
    key_unit, key_inverse = normalize(k_raw)
    queries = rotate(query_unit * head_scales[0], cosine, sine_table).astype(BF16)
    keys = rotate(key_unit * head_scales[1], cosine, sine_table).astype(BF16)
    values = v_raw.astype(BF16)
    text_raw = dot("td,xdk->txk", cap, w_ck).reshape(ts)
    text_unit, text_inverse = normalize(text_raw)
    text_keys = (text_unit * head_scales[2]).astype(BF16)
    text_values = dot("td,xdk->txk", cap, w_cv).reshape(ts).astype(BF16)

    def softmax(scores, live):
        masked = jnp.where(live[None, None, :], scores, NEGATIVE)
        top = jnp.max(masked, axis=-1, keepdims=True)
        e = jnp.exp(masked - top)
        return e / jnp.sum(e, axis=-1, keepdims=True)

    probs = softmax(dot("qhd,khd->hqk", queries, keys) * scaling, key_live)
    own = dot("hqk,khd->qhd", probs.astype(BF16), values)
    text_probs = softmax(dot("qhd,khd->hqk", queries, text_keys) * scaling, text_live)
    other = dot("hqk,khd->qhd", text_probs.astype(BF16), text_values)
    combined = (own + gate_values[None, :, None] * other).astype(BF16).reshape(512, 2, 192)
    attn = z_scatter(dot("sxk,xdk->sd", combined, w_o).astype(BF16), 5)
    unit_two, inverse_two = normalize(attn)
    gate_a = jnp.tanh(gate_attn)
    middle = resid + live_rows * gate_a * unit_two * gains[1]
    unit_three, inverse_three = normalize(middle)
    second_in = (unit_three * gains[2] * (1.0 + scale_ffn)).astype(BF16)
    second_all = z_gather(second_in, 6)
    pre_g = dot("sd,xdf->sxf", second_all, w_g)
    pre_u = dot("sd,xdf->sxf", second_all, w_u)
    sigma = jax.nn.sigmoid(pre_g)
    activated = (pre_g * sigma * pre_u).astype(BF16)
    ffn_total = z_scatter(dot("sxf,xdf->sd", activated, w_dn).astype(BF16), 7)
    unit_four, inverse_four = normalize(ffn_total)
    gate_f = jnp.tanh(gate_ffn)
    layer_out = (middle + live_rows * gate_f * unit_four * gains[3]).astype(BF16)

    weighted = grad_top * live_rows
    gain_four = jnp.sum(weighted * gate_f * unit_four, axis=0)
    gate_ffn_grad = jnp.sum(weighted * unit_four * gains[3], axis=0) * (1.0 - gate_f * gate_f)
    grad_ffn_in = norm_back(unit_four, inverse_four, weighted * gate_f * gains[3]).astype(BF16)
    grad_two = z_gather(grad_ffn_in, 8)
    grad_act = dot("sd,xdf->sxf", grad_two, w_dn)
    down_grad = dot("sd,sxf->xdf", grad_two, activated)
    grad_g = (grad_act * pre_u * sigma * (1.0 + pre_g * (1.0 - sigma))).astype(BF16)
    grad_u = (grad_act * pre_g * sigma).astype(BF16)
    gate_grad = dot("sd,sxf->xdf", second_all, grad_g)
    up_grad = dot("sd,sxf->xdf", second_all, grad_u)
    grad_second = z_scatter(
        (dot("sxf,xdf->sd", grad_g, w_g) + dot("sxf,xdf->sd", grad_u, w_u)).astype(BF16), 9
    )
    scale_ffn_grad = jnp.sum(grad_second * unit_three * gains[2], axis=0)
    gain_three = jnp.sum(grad_second * (1.0 + scale_ffn) * unit_three, axis=0)
    grad_middle = grad_top + norm_back(
        unit_three, inverse_three, grad_second * (1.0 + scale_ffn) * gains[2]
    )
    weighted_mid = grad_middle * live_rows
    gain_two = jnp.sum(weighted_mid * gate_a * unit_two, axis=0)
    gate_attn_grad = jnp.sum(weighted_mid * unit_two * gains[1], axis=0) * (1.0 - gate_a * gate_a)
    grad_attn_in = norm_back(unit_two, inverse_two, weighted_mid * gate_a * gains[1]).astype(BF16)
    grad_one = z_gather(grad_attn_in, 10)
    grad_combined = dot("sd,xdk->sxk", grad_one, w_o).astype(BF16)
    out_grad = dot("sd,sxk->xdk", grad_one, combined)
    grad_heads = grad_combined.reshape(hs)
    gate_local = jnp.sum(grad_heads.astype(F32) * other, axis=(0, 2)) * (
        1.0 - gate_values * gate_values
    )
    grad_text_heads = (gate_values[None, :, None] * grad_heads.astype(F32)).astype(BF16)

    def back(p, grad, vals):
        grad_values = dot("hqk,qhd->khd", p.astype(BF16), grad)
        grad_probs = dot("qhd,khd->hqk", grad, vals)
        grad_scores = p * (grad_probs - jnp.sum(p * grad_probs, axis=-1, keepdims=True))
        return grad_values, grad_scores.astype(BF16)

    grad_values, grad_scores = back(probs, grad_heads, values)
    grad_text_values, grad_text_scores = back(text_probs, grad_text_heads, text_values)
    grad_query = (
        dot("hqk,khd->qhd", grad_scores, keys) + dot("hqk,khd->qhd", grad_text_scores, text_keys)
    ) * scaling
    grad_keys = dot("hqk,qhd->khd", grad_scores, queries) * scaling
    grad_text_keys = dot("hqk,qhd->khd", grad_text_scores, queries) * scaling
    grad_query_rot = rotate_back(grad_query, cosine, sine_table)
    grad_key_rot = rotate_back(grad_keys, cosine, sine_table)
    head_query = jnp.sum(grad_query_rot * query_unit, axis=(0, 1))
    head_key = jnp.sum(grad_key_rot * key_unit, axis=(0, 1))
    head_text = jnp.sum(grad_text_keys * text_unit, axis=(0, 1))
    shape = (512, 2, 192)
    grad_q = norm_back(query_unit, query_inverse, grad_query_rot * head_scales[0])
    grad_k = norm_back(key_unit, key_inverse, grad_key_rot * head_scales[1])
    grad_q = grad_q.astype(BF16).reshape(shape)
    grad_k = grad_k.astype(BF16).reshape(shape)
    grad_v = grad_values.astype(BF16).reshape(shape)
    grad_tk = norm_back(text_unit, text_inverse, grad_text_keys * head_scales[2])
    grad_tk = grad_tk.astype(BF16).reshape(256, 2, 192)
    grad_tv = grad_text_values.astype(BF16).reshape(256, 2, 192)
    grad_first = z_scatter(
        (
            dot("sxk,xdk->sd", grad_q, w_q)
            + dot("sxk,xdk->sd", grad_k, w_k)
            + dot("sxk,xdk->sd", grad_v, w_v)
        ).astype(BF16),
        11,
    )
    scale_attn_grad = jnp.sum(grad_first * unit_one * gains[0], axis=0)
    gain_one = jnp.sum(grad_first * (1.0 + scale_attn) * unit_one, axis=0)
    grad_hidden = grad_middle + norm_back(
        unit_one, inverse_one, grad_first * (1.0 + scale_attn) * gains[0]
    )
    d_grad = jnp.concatenate(
        [
            dot("sd,sxk->xdk", first_all, grad_q).astype(BF16),
            dot("sd,sxk->xdk", first_all, grad_k).astype(BF16),
            dot("sd,sxk->xdk", first_all, grad_v).astype(BF16),
            out_grad.astype(BF16),
            gate_grad.astype(BF16),
            up_grad.astype(BF16),
            down_grad.astype(BF16),
        ],
        axis=2,
    )
    c_grad = jnp.concatenate(
        [
            dot("td,txk->xdk", cap, grad_tk).astype(BF16),
            dot("td,txk->xdk", cap, grad_tv).astype(BF16),
        ],
        axis=2,
    )
    d_out = plane_scatter(d_grad, 12)
    c_out = plane_scatter(c_grad, 13)
    out_half = layer_out.reshape(2, 64, D)
    grad_half = grad_hidden.reshape(2, 64, D)
    out_got, grad_got = kernel_call(
        swap_kernel,
        [out_half, grad_half],
        [S((2, 64, D), BF16), S((2, 64, D), F32)],
        14,
        dma_sems(2),
        name="swap_back",
    )
    mine = jnp.arange(2)[:, None, None] == xl
    layer_final = jnp.where(mine, pick(out_half, xl)[None], pick(out_got, 1 - xl)[None])
    grad_final = jnp.where(mine, pick(grad_half, xl)[None], pick(grad_got, 1 - xl)[None])

    mod_grad = jnp.stack([scale_attn_grad, gate_attn_grad, scale_ffn_grad, gate_ffn_grad])
    mod_msg = jnp.pad(mod_grad.reshape(8, 6, 128), ((0, 0), (0, 2), (0, 0)))
    gain_grad = jnp.stack([gain_one, gain_two, gain_three, gain_four])
    gain_part = jnp.pad(
        jnp.transpose(gain_grad.reshape(4, 16, 96), (1, 0, 2)), ((0, 0), (0, 0), (0, 32))
    )
    gate_part = lax.dynamic_update_slice_in_dim(jnp.zeros((64,), F32), gate_local, z * 6, 0)
    head_part = jnp.concatenate([head_query, head_key, head_text, gate_part]).reshape(2, 128)
    head_part = jnp.broadcast_to(jnp.pad(head_part, ((0, 2), (0, 0)))[None], (16, 4, 128))
    gain_msg = jnp.concatenate([gain_part, head_part], axis=1)
    g_all, gain_out, bias_all = kernel_call(
        small_kernel,
        [mod_msg, gain_msg],
        [S((16, 2, 8, 128), F32), S((8, 128), F32), S((8, 8, 128), F32)],
        15,
        [VMEM((8, 8, 128), F32), VMEM((16, 8, 128), F32), VMEM((8, 8, 128), F32)]
        + dma_sems(7)
        + dma_sems(15)
        + dma_sems(15)
        + dma_sems(7)
        + dma_sems(7),
        name="small_sums",
    )
    g_items = g_all[:, :, :6].reshape(32, 768)
    ada_grad = jnp.einsum("mc,mk->ck", units, g_items, precision=lax.Precision.HIGHEST)
    bias_block = pick(bias_all, dp // 2)[:6].reshape(2, 384)
    bias_grad = pick(bias_block, dp % 2)
    heads = gain_out[4:6].reshape(256)
    return (
        layer_final[:, None],
        grad_final[:, None],
        ada_grad,
        bias_grad,
        gain_out[:4, :96],
        jnp.stack([d_out[:, :192], d_out[:, 192:384], d_out[:, 384:576]]),
        heads[:192].reshape(3, 64),
        jnp.stack([c_out[:, :192], c_out[:, 192:]]),
        heads[192:216],
        d_out[:, 576:768].T,
        jnp.stack([d_out[:, 768:1280], d_out[:, 1280:1792]]),
        d_out[:, 1792:].T,
    )


def solution(mesh):
    return jax.shard_map(
        on_device,
        mesh=mesh,
        in_specs=(
            P(None, "dp", "tensor", None),
            P(None, "dp", None),
            P(None, "dp", None, None),
            P(None, "dp"),
            P(None, "dp"),
            P(None, "dp"),
            P(None, "dp"),
            P(None, "dp", "tensor", None),
            P("dp", "tensor"),
            P("dp"),
            P(None, "dp"),
            P(None, "dp", "tensor"),
            P(),
            P(None, "dp", "tensor"),
            P(),
            P("tensor", "dp"),
            P(None, "dp", "tensor"),
            P("tensor", "dp"),
        ),
        out_specs=(
            P(None, "dp", "tensor", None),
            P(None, "dp", "tensor", None),
            P("dp", "tensor"),
            P("dp"),
            P(None, "dp"),
            P(None, "dp", "tensor"),
            P(),
            P(None, "dp", "tensor"),
            P(),
            P("tensor", "dp"),
            P(None, "dp", "tensor"),
            P("tensor", "dp"),
        ),
        check_vma=False,
    )
```

time: 1800 us -> 707 us (0.39)
  waiting for transfers between devices: 1280 us -> 0 us
  Pallas kernels: 0 us -> 408 us
  blocking collectives: 223 us -> 0 us
  local copies, waits for them, and re-layouts: 67.6 us -> 101 us
  between operations: 27.1 us -> 6.5 us
    reduce_scatter x11 -> x0, waiting for transfers between devices: 565 us -> none  [the longest x2 139 us: on_device(): lax.psum_scatter(jnp.einsum('csf,cdf->sd', grad_pre, full_ffn, preferred_...]
    all_gather x13 -> x0, waiting for transfers between devices: 412 us -> none  [the longest x2 79.7 us: on_device(): gathered_two = lax.all_gather(second_in, 'tensor', axis=0, tiled=True)]
    pallas_call x0 -> x15, Pallas kernels: none -> 408 us  [kernel_call(): pl.pallas_call(body, out_shape=out_shape, in_specs=[pl.BlockSpec(memory_s...]
    unnamed x32 -> x0, waiting for transfers between devices: 306 us -> none
    all_gather x4 -> x0, blocking collectives: 100 us -> none  [the longest x1 32.5 us: on_device(): lax.all_gather(out_weight, 'dp', axis=1, tiled=True)]
    psum x2 -> x0, blocking collectives: 63.1 us -> none  [the longest x1 36.1 us: on_device(): head_done, gate_done = lax.psum((head_total, gate_total), 'dp')]
    unnamed x1 -> x0, blocking collectives: 60.1 us -> none
    concatenate x0 -> x3, local copies, waits for them, and re-layouts: none -> 27.1 us  [the longest x1 17.5 us: on_device(): jnp.concatenate([dot('sd,sxk->xdk', first_all, grad_q).astype(BF16), dot(...]
  transfers between devices with their start and end apart: 28 -> 0, of which waited for: 26 -> 0; matrix products, arithmetic and copies ran while one was open for 10% -> 0% of each run, Pallas kernels for 0% -> 0%
where the time goes in v1:
time: 707 us; the launch traced here: 699 us
  Pallas kernels  408 us (58%)
  matrix products  112 us (16%)
  local copies, waits for them, and re-layouts  101 us (14%)
  other arithmetic  71.7 us (10%)
    pallas_call x15, Pallas kernels, kernel_call(): pl.pallas_call(body, out_shape=out_shape, in_specs=[pl.BlockSpec(memory_s...  408 us
    dot_general x34, matrix products, dot(): return jnp.einsum(spec, a, b, preferred_element_type=F32)  97.6 us
    dot_general x6, local copies, waits for them, and re-layouts, dot(): return jnp.einsum(spec, a, b, preferred_element_type=F32)  22.1 us
    concatenate x1, local copies, waits for them, and re-layouts, on_device(): jnp.concatenate([dot('sd,sxk->xdk', first_all, grad_q).astype(BF16), dot(...  17.5 us
    unnamed x197, local copies, waits for them, and re-layouts  17 us

profile of v1, /device:TPU:1, one launch (start us, length us, event | category | flops | bytes accessed | tf_op | source)
XLA Modules:
  0.0 699.3 jit_solution(16276486119281604857)
XLA Ops:
  25.1 25.7 %modulation.1 = (f32[16,8,128]{2,1,0:T(8,128)}, f32[8,8,768]{2,1,0:T(8,128)}) custom-call(f32[16,8,128]{2,1,0:T(8,128)} %pad_maximum_fusion.16.msg_ref, bf16[128,768]{1,0:T(8,128)(2,1)} %pad.36.ada_ref, f32[1,768]{1,0:T(1,128)} %broadcast_in_dim.136.bias_ref), custom_call_target="tpu_custom_call" | custom-call | tf_op jit(solution)/shard_map/modulation/pallas_call | solution.py:70
  61.7 21.1 %hidden_gather.1 = (bf16[4,2,64,1536]{3,2,1,0:T(8,128)(2,1)}, bf16[2,64,1536]{2,1,0:T(8,128)(2,1)}) custom-call(bf16[2,64,1536]{2,1,0:T(8,128)(2,1)} %bitcast.371, bf16[2,64,1536]{2,1,0:T(8,128)(2,1)} %bitcast.372), custom_call_target="tpu_custom_call" | custom-call | tf_op jit(solution)/shard_map/hidden_gather/pallas_call | solution.py:70
  89.4 39.0 %plane_gather4.1 = bf16[2,2,4,2,256,384]{5,4,3,2,1,0:T(8,128)(2,1)} custom-call(bf16[256,384]{1,0:T(8,128)(2,1)} %pad_maximum_fusion.8.w_ref), custom_call_target="tpu_custom_call" | custom-call | tf_op jit(solution)/shard_map/plane_gather4/pallas_call | solution.py:70
  128.5 6.8 slice_bitcast_fusion
  151.3 62.2 %plane_gather3.1 = bf16[2,2,4,2,96,2304]{5,4,3,2,1,0:T(8,128)(2,1)} custom-call(bf16[96,2304]{1,0:T(8,128)(2,1)} %concatenate.45.w_ref), custom_call_target="tpu_custom_call" | custom-call | tf_op jit(solution)/shard_map/plane_gather3/pallas_call | solution.py:70
  213.5 6.7 fusion.153
  245.4 6.8 fusion.156
  261.2 19.1 %z_scatter5.1 = f32[128,1536]{1,0:T(8,128)} custom-call(bf16[4,128,1536]{2,1,0:T(8,128)(2,1)} %bitcast.344), custom_call_target="tpu_custom_call" | custom-call | tf_op jit(solution)/shard_map/z_scatter5/pallas_call | solution.py:70
  284.1 16.9 %z_gather6.1 = bf16[4,128,1536]{2,1,0:T(8,128)(2,1)} custom-call(bf16[128,1536]{1,0:T(8,128)(2,1)} %multiply_convert_fusion.8.x_ref), custom_call_target="tpu_custom_call" | custom-call | tf_op jit(solution)/shard_map/z_gather6/pallas_call | solution.py:70
  305.4 5.9 multiply_convert_fusion.4
  316.5 16.3 %z_scatter7.1 = f32[128,1536]{1,0:T(8,128)} custom-call(bf16[4,128,1536]{2,1,0:T(8,128)(2,1)} %bitcast.345), custom_call_target="tpu_custom_call" | custom-call | tf_op jit(solution)/shard_map/z_scatter7/pallas_call | solution.py:70
  334.2 11.7 %fusion.90 = (f32[1536]{0:T(1024)S(1)}, f32[128]{0:T(128)S(1)}, f32[1536]{0:T(1024)S(1)}) fusion(f32[128,1536]{1,0:T(8,128)} %z_scatter7.1, bf16[2,64,1536]{2,1,0:T(8,128)(2,1)S(1)} %copy-done.11, f32[128]{0:T(128)S(1)} %add_rsqrt_fusion.5, f32[1536]{0:T(1024)S(1)} %copy-done.54, f32[128]{0:T(128)S(1)} %compare_convert_fusion, f32[1536]{0:T(1024)S(1)} %copy-done.55), kind=kLoop, calls=%fused_computation.127 | loop fusion | flops 2356096 | bytes 1205760 | tf_op jit(solution)/shard_map/reduce_sum | solution.py:697
  350.4 16.4 %z_gather8.1 = bf16[4,128,1536]{2,1,0:T(8,128)(2,1)} custom-call(bf16[128,1536]{1,0:T(8,128)(2,1)} %get-tuple-element.118.x_ref), custom_call_target="tpu_custom_call" | custom-call | tf_op jit(solution)/shard_map/z_gather8/pallas_call | solution.py:70
  366.8 5.4 multiply_convert_fusion.3
  381.7 14.0 %z_scatter9.1 = f32[128,1536]{1,0:T(8,128)} custom-call(bf16[4,128,1536]{2,1,0:T(8,128)(2,1)} %bitcast.343), custom_call_target="tpu_custom_call" | custom-call | tf_op jit(solution)/shard_map/z_scatter9/pallas_call | solution.py:70
  410.2 17.4 %z_gather10.1 = bf16[4,128,1536]{2,1,0:T(8,128)(2,1)} custom-call(bf16[128,1536]{1,0:T(8,128)(2,1)} %multiply_convert_fusion.7.x_ref), custom_call_target="tpu_custom_call" | custom-call | tf_op jit(solution)/shard_map/z_gather10/pallas_call | solution.py:70
  443.4 8.6 %copy.114 = bf16[2,4096,384]{2,1,0:T(8,128)(2,1)} copy(bf16[2,4096,384]{1,2,0:T(8,128)(2,1)} %pad_maximum_fusion) | data formatting | bytes 12582912 | tf_op jit(solution)/shard_map/concatenate | solution.py:780
  452.0 41.0 %plane_scatter13.1 = f32[256,384]{1,0:T(8,128)} custom-call(bf16[2,2,4,2,256,384]{5,4,3,2,1,0:T(8,128)(2,1)} %bitcast.323), custom_call_target="tpu_custom_call" | custom-call | tf_op jit(solution)/shard_map/plane_scatter13/pallas_call | solution.py:70
  499.7 6.6 multiply_reduce_fusion
  521.4 18.0 %z_scatter11.1 = f32[128,1536]{1,0:T(8,128)} custom-call(bf16[4,128,1536]{2,1,0:T(8,128)(2,1)} %bitcast.324), custom_call_target="tpu_custom_call" | custom-call | tf_op jit(solution)/shard_map/z_scatter11/pallas_call | solution.py:70
  546.2 19.7 %small_sums.1 = (f32[16,2,8,128]{3,2,1,0:T(8,128)}, f32[8,128]{1,0:T(8,128)}, f32[8,8,128]{2,1,0:T(8,128)}) custom-call(f32[8,8,128]{2,1,0:T(8,128)} %pad.37.mod_ref, f32[16,8,128]{2,1,0:T(8,128)} %select_maximum_fusion.gain_ref), custom_call_target="tpu_custom_call" | custom-call | tf_op jit(solution)/shard_map/small_sums/pallas_call | solution.py:70
  572.4 16.2 %swap_back.1 = (bf16[2,64,1536]{2,1,0:T(8,128)(2,1)}, f32[2,64,1536]{2,1,0:T(8,128)}) custom-call(bf16[2,64,1536]{2,1,0:T(8,128)(2,1)} %bitcast.334, f32[2,64,1536]{2,1,0:T(8,128)} %bitcast.330), custom_call_target="tpu_custom_call" | custom-call | tf_op jit(solution)/shard_map/swap_back/pallas_call | solution.py:70
  610.5 17.5 %copy.112 = bf16[2,1536,2304]{2,1,0:T(8,128)(2,1)} copy(bf16[2,1536,2304]{1,2,0:T(8,128)(2,1)} %fusion.10) | data formatting | bytes 28311552 | tf_op jit(solution)/shard_map/concatenate | solution.py:768
  628.1 65.4 %plane_scatter12.1 = f32[96,2304]{1,0:T(8,128)} custom-call(bf16[2,2,4,2,96,2304]{5,4,3,2,1,0:T(8,128)(2,1)} %bitcast.310), custom_call_target="tpu_custom_call" | custom-call | tf_op jit(solution)/shard_map/plane_scatter12/pallas_call | solution.py:70
  (362 shorter events, 208.2 us)
Async XLA Ops:
  0.7 60.1 %copy-start.53 = (bf16[512,96]{0,1:T(8,128)(2,1)S(1)}, bf16[512,96]{0,1:T(8,128)(2,1)}, u32[]{:S(2)}) copy-start(bf16[512,96]{0,1:T(8,128)(2,1)} %param.35) | copy-start | bytes 294916
  0.7 60.1 %copy-start.42 = (bf16[2,96,512]{2,1,0:T(8,128)(2,1)S(1)}, bf16[2,96,512]{2,1,0:T(8,128)(2,1)}, u32[]{:S(2)}) copy-start(bf16[2,96,512]{2,1,0:T(8,128)(2,1)} %param.34) | copy-start | bytes 589828
  58.8 30.7 %copy-start.46 = (f32[1536]{0:T(1024)}, f32[1536]{0:T(1024)S(1)}, u32[]{:S(2)}) copy-start(f32[1536]{0:T(1024)S(1)} %mul.801) | copy-start | bytes 18436
  256.7 25.0 %copy-start.3 = (bf16[4,2,64,1536]{3,2,1,0:T(8,128)(2,1)S(1)}, bf16[4,2,64,1536]{3,2,1,0:T(8,128)(2,1)}, u32[]{:S(2)}) copy-start(bf16[4,2,64,1536]{3,2,1,0:T(8,128)(2,1)} %get-tuple-element.21) | copy-start | bytes 4718596
  256.7 25.0 %copy-start.43 = (f32[1536]{0:T(1024)S(1)}, f32[1536]{0:T(1024)}, u32[]{:S(2)}) copy-start(f32[1536]{0:T(1024)} %tanh.42) | copy-start | bytes 18436
  256.7 25.0 %copy-start.50 = (f32[1536]{0:T(1024)S(1)}, f32[1536]{0:T(1024)}, u32[]{:S(2)}) copy-start(f32[1536]{0:T(1024)} %mul.849) | copy-start | bytes 18436
  261.2 22.0 %copy-start.44 = (f32[1536]{0:T(1024)S(1)}, f32[1536]{0:T(1024)}, u32[]{:S(2)}) copy-start(f32[1536]{0:T(1024)} %add.267) | copy-start | bytes 18436
  261.2 22.0 %copy-start.51 = (f32[1536]{0:T(1024)S(1)}, f32[1536]{0:T(1024)}, u32[]{:S(2)}) copy-start(f32[1536]{0:T(1024)} %mul.857) | copy-start | bytes 18436
  281.6 23.7 %copy-start.68 = (f32[128]{0:T(128)}, f32[128]{0:T(128)S(1)}, u32[]{:S(2)}) copy-start(f32[128]{0:T(128)S(1)} %add_rsqrt_fusion.7) | copy-start | bytes 1540
  283.2 22.1 %copy-start.66 = (f32[128]{0:T(128)}, f32[128]{0:T(128)S(1)}, u32[]{:S(2)}) copy-start(f32[128]{0:T(128)S(1)} %add_rsqrt_fusion.6) | copy-start | bytes 1540
  316.5 29.3 %copy-start.59 = (f32[2,1,768]{2,1,0:T(1,128)S(1)}, f32[2,1,768]{2,1,0:T(1,128)}, u32[]{:S(2)}) copy-start(f32[2,1,768]{2,1,0:T(1,128)} %get-tuple-element.134) | copy-start | bytes 18436
  349.6 22.6 %copy-start.14 = (bf16[128,1536]{1,0:T(8,128)(2,1)}, bf16[128,1536]{1,0:T(8,128)(2,1)S(1)}, u32[]{:S(2)}) copy-start(bf16[128,1536]{1,0:T(8,128)(2,1)S(1)} %get-tuple-element.119) | copy-start | bytes 1179652
  406.0 21.6 %copy-start.28 = (bf16[2,1536,192]{1,2,0:T(8,128)(2,1)S(1)}, bf16[2,1536,192]{1,2,0:T(8,128)(2,1)}, u32[]{:S(2)}) copy-start(bf16[2,1536,192]{1,2,0:T(8,128)(2,1)} %copy.133) | copy-start | bytes 3538948
  517.7 21.7 %copy-start.47 = (f32[1536]{0:T(1024)S(1)}, f32[1536]{0:T(1024)}, u32[]{:S(2)}) copy-start(f32[1536]{0:T(1024)} %copy-done.46) | copy-start | bytes 18436
  517.7 21.7 %copy-start.71 = (f32[128]{0:T(128)S(1)}, f32[128]{0:T(128)}, u32[]{:S(2)}) copy-start(f32[128]{0:T(128)} %rsqrt.75) | copy-start | bytes 1540
  521.4 20.3 %copy-start.56 = (f32[1,16,96]{2,0,1:T(1,128)S(1)}, f32[1,16,96]{2,0,1:T(1,128)}, u32[]{:S(2)}) copy-start(f32[1,16,96]{2,0,1:T(1,128)} %stack.62) | copy-start | bytes 18436
  521.4 20.3 %copy-start.57 = (f32[1,16,96]{2,0,1:T(1,128)S(1)}, f32[1,16,96]{2,0,1:T(1,128)}, u32[]{:S(2)}) copy-start(f32[1,16,96]{2,0,1:T(1,128)} %stack.61) | copy-start | bytes 18436
  521.4 20.4 %copy-start.58 = (f32[1,16,96]{2,0,1:T(1,128)S(1)}, f32[1,16,96]{2,0,1:T(1,128)}, u32[]{:S(2)}) copy-start(f32[1,16,96]{2,0,1:T(1,128)} %stack.60) | copy-start | bytes 18436
  521.4 21.1 %copy-start.4 = (f32[128,1536]{1,0:T(8,128)S(1)}, f32[128,1536]{1,0:T(8,128)}, u32[]{:S(2)}) copy-start(f32[128,1536]{1,0:T(8,128)} %get-tuple-element.92) | copy-start | bytes 2359300
  542.4 48.2 %copy-start.70 = (pred[2]{0:T(512)(128)(4,1)S(1)}, pred[2]{0:T(512)(128)(4,1)}, u32[]{:S(2)}) copy-start(pred[2]{0:T(512)(128)(4,1)} %iota_compare_fusion.5) | copy-start | bytes 10
  543.9 28.5 %copy-start.9 = (f32[128,1536]{1,0:T(8,128)}, f32[128,1536]{1,0:T(8,128)S(1)}, u32[]{:S(2)}) copy-start(f32[128,1536]{1,0:T(8,128)S(1)} %fusion.102) | copy-start | bytes 2359300
  543.9 47.7 %copy-start.32 = (bf16[64,1536]{1,0:T(8,128)(2,1)S(1)}, bf16[64,1536]{1,0:T(8,128)(2,1)}, u32[]{:S(2)}) copy-start(bf16[64,1536]{1,0:T(8,128)(2,1)} %dynamic-slice_bitcast_fusion.3) | copy-start | bytes 589828
  543.9 48.6 %copy-start.19 = (bf16[4,2,64,1536]{3,2,1,0:T(8,128)(2,1)S(1)}, bf16[4,2,64,1536]{3,2,1,0:T(8,128)(2,1)}, u32[]{:S(2)}) copy-start(bf16[4,2,64,1536]{3,2,1,0:T(8,128)(2,1)} %fusion.17) | copy-start | bytes 4718596
  628.1 70.7 %copy-start.1 = (s32[2,1]{0,1:T(1,128)S(1)}, s32[2,1]{0,1:T(1,128)}, u32[]{:S(2)}) copy-start(s32[2,1]{0,1:T(1,128)} %param.24) | copy-start | bytes 28
  (71 other events, 350.7 us)

commit v2 on v1

--- a/solution.py
+++ b/solution.py
@@ -543,6 +543,853 @@
     return rotate(gradient, cosine, -sine_table)
 
 
+def z_ring():
+    xh, xl, y, z, c = coords()
+    x = 2 * xh + xl
+    return z, device_of(x, y, (z + 1) % 4, c), device_of(x, y, (z + 3) % 4, c)
+
+
+class ZGather:
+    def __init__(self, send, own, every, right, left):
+        self.send, self.every, self.right, self.left = send, every, right, left
+        self.from_left = send(own, every.at[1], right)
+        self.from_right = send(own, every.at[2], left)
+
+    def near(self):
+        self.from_left.wait_recv()
+        every = self.every
+        half = every.shape[1] // 2
+        lower, upper = pl.ds(0, half), pl.ds(half, half)
+        self.far_low = self.send(every.at[1, lower], every.at[3, lower], self.right)
+        self.from_right.wait_recv()
+        self.far_up = self.send(every.at[2, upper], every.at[3, upper], self.left)
+
+    def far(self):
+        self.far_low.wait_recv()
+        self.far_up.wait_recv()
+
+
+class ZScatter:
+    def __init__(self, send, part, relay, got, right, left):
+        self.send, self.part, self.relay, self.got = send, part, relay, got
+        self.right, self.left = right, left
+        half = part.shape[1] // 2
+        self.lower, self.upper = pl.ds(0, half), pl.ds(half, half)
+
+    def near(self):
+        part, got = self.part, self.got
+        self.near_r = self.send(part.at[2, self.upper], got.at[0, self.upper], self.right)
+        self.near_l = self.send(part.at[1, self.lower], got.at[1, self.lower], self.left)
+
+    def far(self):
+        part, relay = self.part, self.relay
+        self.relay_r = self.send(part.at[3, self.lower], relay.at[0], self.right)
+        self.relay_l = self.send(part.at[3, self.upper], relay.at[1], self.left)
+
+    def pass_on(self):
+        part, relay, got = self.part, self.relay, self.got
+        self.relay_r.wait_recv()
+        part[2, self.lower] = add_low(part[2, self.lower], relay[0])
+        self.last_r = self.send(part.at[2, self.lower], got.at[0, self.lower], self.right)
+        self.relay_l.wait_recv()
+        part[1, self.upper] = add_low(part[1, self.upper], relay[1])
+        self.last_l = self.send(part.at[1, self.upper], got.at[1, self.upper], self.left)
+
+    def total(self):
+        for copy in (self.near_r, self.near_l, self.last_r, self.last_l):
+            copy.wait_recv()
+        got = self.got
+        return self.part[0].astype(F32) + got[0].astype(F32) + got[1].astype(F32)
+
+
+def mm(a, b):
+    return lax.dot_general(a, b, (((1,), (0,)), ((), ())), preferred_element_type=F32)
+
+
+def mm_t(a, b):
+    return lax.dot_general(a, b, (((1,), (1,)), ((), ())), preferred_element_type=F32)
+
+
+def tile(j, size=256):
+    return pl.ds(pl.multiple_of(j * size, size), size)
+
+
+def transpose_into(src, dst):
+    def column(j, carry):
+        cols = tile(j, 128)
+        for slot in range(4):
+            dst[cols, slot * 128 : (slot + 1) * 128] = src[slot, :, cols].T
+        return carry
+
+    lax.fori_loop(0, D // 128, column, 0)
+
+
+class PlaneGather:
+    def __init__(self, send, shard, every):
+        self.send, self.shard, self.every = send, shard, every
+        rows, cols = shard.shape
+        half = rows // 2
+        self.top, self.low = pl.ds(0, half), pl.ds(half, half)
+        if rows == 96:
+            left, right = pl.ds(0, cols // 2), pl.ds(cols // 2, cols // 2)
+            self.qa = [(self.top, left), (self.top, right)]
+            self.qb = [(self.low, left), (self.low, right)]
+        else:
+            q = half // 2
+            self.qa = [(pl.ds(0, q),), (pl.ds(q, q),)]
+            self.qb = [(pl.ds(2 * q, q),), (pl.ds(3 * q, q),)]
+        self.late = []
+
+    def at(self, xx, yy, *rest):
+        return self.every.at[(xx % 2, xx // 2, yy, self.c) + rest]
+
+    def same(self, ref, device):
+        return self.send(ref, ref, device)
+
+    def to_sibling(self, ref):
+        self.late.append(self.send(ref, ref, self.sibling))
+
+    def start(self, local_sem):
+        x, y, c, xr, xq, yr, yq, peers = plane_peers()
+        self.x, self.y, self.c = x, y, c
+        self.xr, self.xq, self.yr, self.yq = xr, xq, yr, yq
+        self.go_xr, self.go_xq, self.go_yr, self.go_yq, self.sibling = peers
+        shard, top, low = self.shard, self.top, self.low
+        self.a_r = self.send(shard.at[top], self.at(x, y, top), self.go_xr)
+        self.a_l = self.send(shard.at[top], self.at(x, y, top), self.go_xq)
+        self.b_r = self.send(shard.at[low], self.at(x, y, low), self.go_yr)
+        self.b_l = self.send(shard.at[low], self.at(x, y, low), self.go_yq)
+        self.late.append(self.send(shard, self.at(x, y), self.sibling))
+        self.local = pltpu.make_async_copy(shard, self.at(x, y), local_sem)
+        self.local.start()
+
+    def step2(self):
+        x, y = self.x, self.y
+        self.a_r.wait_recv()
+        self.f1 = self.same(self.at(self.xq, y, *self.qa[0]), self.go_xr)
+        self.a_l.wait_recv()
+        self.f2 = self.same(self.at(self.xr, y, *self.qa[1]), self.go_xq)
+        self.b_r.wait_recv()
+        self.f3 = self.same(self.at(x, self.yq, *self.qb[0]), self.go_yr)
+        self.b_l.wait_recv()
+        self.f4 = self.same(self.at(x, self.yr, *self.qb[1]), self.go_yq)
+
+    def step3(self):
+        x, y, c = self.x, self.y, self.c
+        every, top, low = self.every, self.top, self.low
+        self.local.wait()
+        self.f1.wait_recv()
+        self.f2.wait_recv()
+        block = every.at[:, :, y, c, top]
+        self.g_r = self.same(block, self.go_yr)
+        self.g_l = self.same(block, self.go_yq)
+        self.f3.wait_recv()
+        self.f4.wait_recv()
+        block = every.at[x % 2, x // 2, :, c, low]
+        self.h_r = self.same(block, self.go_xr)
+        self.h_l = self.same(block, self.go_xq)
+        for k in range(1, 4):
+            self.to_sibling(self.at((x + k) % 4, y, top))
+            self.to_sibling(self.at(x, (y + k) % 4, low))
+
+    def step4(self):
+        c, every, top, low = self.c, self.every, self.top, self.low
+        xr, xq, yr, yq = self.xr, self.xq, self.yr, self.yq
+        self.g_r.wait_recv()
+        self.f1 = self.same(every.at[0, :, yq, c, top], self.go_yr)
+        self.g_l.wait_recv()
+        self.f2 = self.same(every.at[1, :, yr, c, top], self.go_yq)
+        self.h_r.wait_recv()
+        self.f3 = self.same(every.at[xq % 2, xq // 2, pl.ds(0, 2), c, low], self.go_xr)
+        self.h_l.wait_recv()
+        self.f4 = self.same(every.at[xr % 2, xr // 2, pl.ds(2, 2), c, low], self.go_xq)
+        self.to_sibling(every.at[:, :, yq, c, top])
+        self.to_sibling(every.at[:, :, yr, c, top])
+        self.to_sibling(every.at[xq % 2, xq // 2, :, c, low])
+        self.to_sibling(every.at[xr % 2, xr // 2, :, c, low])
+
+    def step5(self):
+        c, every, top, low = self.c, self.every, self.top, self.low
+        xo, yo = (self.x + 2) % 4, (self.y + 2) % 4
+        for copy in (self.f1, self.f2, self.f3, self.f4):
+            copy.wait_recv()
+        self.to_sibling(every.at[:, :, yo, c, top])
+        self.to_sibling(every.at[xo % 2, xo // 2, :, c, low])
+
+    def finish(self):
+        for copy in self.late:
+            copy.wait_recv()
+
+
+OFFSETS = (0, 3, 1, 2)
+
+
+def lanes(shape):
+    return lax.broadcasted_iota(jnp.int32, shape, len(shape) - 1)
+
+
+def head_block():
+    row = lax.broadcasted_iota(jnp.int32, (128, 128), 0) // 64
+    col = lax.broadcasted_iota(jnp.int32, (128, 128), 1) // 64
+    return jnp.where(row == col, 1.0 / 64.0, 0.0).astype(BF16)
+
+
+def head_mean(values, block):
+    high = values.astype(BF16)
+    low = (values - high.astype(F32)).astype(BF16)
+    return mm(high, block) + mm(low, block)
+
+
+def swap_quarters(values):
+    second = (lanes(values.shape) % 64) >= 32
+    return jnp.where(second, pltpu.roll(values, 32, 1), pltpu.roll(values, 96, 1))
+
+
+def pick_scalar(ref, xl):
+    return jnp.where(xl == 0, ref[0, 0], ref[1, 0])
+
+
+def key_bias(total, z, length):
+    lane = lanes((1, total))
+    if total == 512:
+        slot = lane // 128
+        block = jnp.where(slot == 0, z, jnp.where(slot == 1, z + 3, jnp.where(slot == 2, z + 1, z + 2)))
+        position = (block % 4) * 128 + lane % 128
+    else:
+        position = lane
+    return jnp.where(position < length, 0.0, NEGATIVE)
+
+
+def fill_rope(cos_ref, sin_ref, z, length, frames, width):
+    lane = lanes((128, 128))
+    pair = lane % 32
+    offset = jnp.where(pair >= 20, 20, jnp.where(pair >= 8, 8, 0))
+    size = jnp.where(pair >= 8, 12.0, 8.0)
+    freq = jnp.exp((pair - offset).astype(F32) / size * (-9.210340371976184))
+    sign = jnp.where(lane % 64 >= 32, 1.0, -1.0)
+    ones = jnp.ones((128, 128), F32)
+    count = ones * length.astype(F32)
+    frame_count = ones * frames.astype(F32)
+    row_size = ones * width.astype(F32)
+    per_frame = jnp.floor((count + frame_count - 0.5) / frame_count)
+    row = lax.broadcasted_iota(jnp.int32, (128, 128), 0).astype(F32)
+    for slot in range(4):
+        start = (((z + OFFSETS[slot]) % 4) * 128).astype(F32)
+        position = row + start
+        frame = jnp.floor((position + 0.5) / per_frame)
+        within = position - frame * per_frame
+        row_pos = jnp.floor((within + 0.5) / row_size)
+        col_pos = within - row_pos * row_size
+        chosen = jnp.where(pair >= 20, col_pos, jnp.where(pair >= 8, row_pos, frame))
+        angle = chosen * freq
+        cos_ref[slot] = jnp.cos(angle)
+        sin_ref[slot] = jnp.sin(angle) * sign
+
+
+def attention_kernel(
+    hid_ref,
+    cot_ref,
+    cond_ref,
+    gain_in,
+    bias_in,
+    ada_ref,
+    qkv_ref,
+    out_t_ref,
+    ffn_w_ref,
+    down_t_ref,
+    cap_w_ref,
+    cap_hbm,
+    hg_ref,
+    gate_ref,
+    len_ref,
+    frame_ref,
+    width_ref,
+    tlen_ref,
+    w_a,
+    w_f,
+    first,
+    resid_ref,
+    cot_out,
+    q8,
+    kk,
+    vv,
+    qr,
+    kr,
+    tk,
+    tv,
+    tkr,
+    other_ref,
+    lse_ref,
+    cw,
+    attn_ref,
+    mid_ref,
+    second_ref,
+    mod_ref,
+    gains_ref,
+    got1,
+    cos_ref,
+    sin_ref,
+    live_ref,
+    sh_a,
+    sh_f,
+    sh_c,
+    w_c,
+    cap,
+    hid_all,
+    hid_own,
+    msg,
+    sent2,
+    got2,
+    got3,
+    mixed,
+    text_acc,
+    part,
+    relay,
+    got,
+    local_sems,
+    ss,
+    rs,
+):
+    dp = lax.axis_index("dp")
+    t = lax.axis_index("tensor")
+    xh, xl, y, z, c = coords()
+    _, right, left = z_ring()
+    pair = device_of(2 * xh + 1 - xl, y, z, c)
+    dp_peers = [((dp + k) % 16, t) for k in range(1, 16)]
+    t_peers = [(dp, (t + k) % 8) for k in range(1, 8)]
+    outer_x = device_of((2 * xh + xl + 3 - 2 * xl) % 4, y, z, c)
+    barrier = pltpu.get_barrier_semaphore()
+    everyone = dp_peers + t_peers + [outer_x]
+    for device in everyone:
+        pl.semaphore_signal(barrier, inc=1, device_id=device, device_id_type=MESH)
+    load_cap = pltpu.make_async_copy(cap_hbm.at[xl], cap, local_sems.at[0])
+    load_cap.start()
+    qs, ks, vs = qkv_ref[0], qkv_ref[1], qkv_ref[2]
+    os = out_t_ref[...]
+    sh_a[...] = jnp.concatenate(
+        [
+            qs,
+            ks[:, 128:192],
+            ks[:, 0:128],
+            vs,
+            os[:, 128:192],
+            os[:, 0:128],
+        ],
+        axis=1,
+    )
+    ck, cv = cap_w_ref[0], cap_w_ref[1]
+    sh_c[...] = jnp.concatenate([ck, cv[:, 128:192], cv[:, 0:128]], axis=1)
+    unit = swish(cond_ref[...].astype(F32)).astype(BF16).astype(F32)
+    msg[...] = jnp.zeros((16, 8, 128), F32)
+    gain_rows = gain_in[...].astype(F32)
+    for d in range(16):
+        msg[d, 0:2, 0:64] = unit[:, d * 64 : (d + 1) * 64]
+        msg[d, 4:8, 0:96] = gain_rows
+    pl.semaphore_wait(barrier, len(everyone))
+
+    send = Sender(ss, rs)
+    swap = send(hid_ref.at[1 - xl], hid_own.at[xl], pair)
+    cot_swap = send(cot_ref.at[1 - xl], cot_out.at[xl], pair)
+    round1 = [send(msg.at[p[0]], got1.at[dp], p) for p in dp_peers]
+    ga = PlaneGather(send, sh_a, w_a)
+    gc = PlaneGather(send, sh_c, w_c)
+    gf = PlaneGather(send, sh_f, w_f)
+    ga.start(local_sems.at[1])
+    hid_own[xl] = hid_ref[xl]
+    cot_out[xl] = cot_ref[xl]
+    got1[dp] = msg[dp]
+    sh_f[:, 0:512] = ffn_w_ref[0]
+    sh_f[:, 512:1024] = ffn_w_ref[1]
+    sh_f[:, 1024:1536] = down_t_ref[...]
+    length = pick_scalar(len_ref, xl)
+    text_len = pick_scalar(tlen_ref, xl)
+    swap.wait_recv()
+    tokens = ZGather(send, hid_own, hid_all, right, left)
+    hid_all[0] = hid_own[...]
+    gc.start(local_sems.at[2])
+    for copy in round1:
+        copy.wait_recv()
+    rows = got1[...].reshape(128, 128)[:, :64].astype(BF16)
+    bias = bias_in[...].astype(F32)
+    here = t == dp // 2
+    low_bias = jnp.where(jnp.logical_and(here, dp % 2 == 0), 1.0, 0.0)
+    high_bias = jnp.where(jnp.logical_and(here, dp % 2 == 1), 1.0, 0.0)
+    terms = mm(rows, ada_ref[...])
+    terms = terms + jnp.concatenate([bias * low_bias, bias * high_bias], axis=1)
+    sent2[...] = jnp.zeros((16, 16, 128), F32)
+    for d in range(16):
+        for j in range(6):
+            sent2[d, 2 * j : 2 * j + 2, :] = terms[8 * d : 8 * d + 2, 128 * j : 128 * j + 128]
+    round2 = [send(sent2.at[p[0]], got2.at[dp], p) for p in dp_peers]
+    got2[dp] = sent2[dp]
+    ga.step2()
+    fill_rope(cos_ref, sin_ref, z, length, pick_scalar(frame_ref, xl), pick_scalar(width_ref, xl))
+    gc.step2()
+    ga.step3()
+    tokens.near()
+    for copy in round2:
+        copy.wait_recv()
+    got3[t] = jnp.sum(got2[...], axis=0)
+    round3 = [send(got3.at[t], got3.at[t], p) for p in t_peers]
+    for d in range(16):
+        gains_ref[0:4, d * 96 : (d + 1) * 96] = got1[d, 4:8, 0:96]
+    gains_ref[4:8, :] = jnp.zeros((4, D), F32)
+    slot_row = lax.broadcasted_iota(jnp.int32, (128, 128), 0) + z * 128
+    live_ref[...] = jnp.where(slot_row < length, 1.0, 0.0)
+    gc.step3()
+    ga.step4()
+    gf.start(local_sems.at[3])
+    for copy in round3:
+        copy.wait_recv()
+    for i in range(4):
+        for h in range(2):
+            block = got3[2 * i + h]
+            for j in range(6):
+                lo = h * 768 + j * 128
+                mod_ref[i : i + 1, lo : lo + 128] = jnp.where(
+                    xl == 0, block[2 * j : 2 * j + 1], block[2 * j + 1 : 2 * j + 2]
+                )
+    mod_ref[4:8, :] = jnp.zeros((4, D), F32)
+    factor = gains_ref[0:1, :] * (1.0 + mod_ref[0:1, :])
+    tokens.far()
+
+    def scale_rows(slot, carry):
+        unit_rows, _ = normalize(hid_all[slot].reshape(128, D).astype(F32))
+        first[slot] = (unit_rows * factor).astype(BF16)
+        return carry
+
+    lax.fori_loop(0, 4, scale_rows, 0)
+    resid_ref[...] = hid_all[0].reshape(128, D)
+    gc.step4()
+    ga.step5()
+    gf.step2()
+    ga.finish()
+
+    x_rows = first[...].reshape(512, D)
+    low_head = lanes((512, 128)) < 64
+    w_flat = w_a
+
+    def project(xx, cols):
+        w_cols = w_flat[xx, :, :, :, :, cols].reshape(D, cols.stop - cols.start)
+        return mm(x_rows, w_cols)
+
+    for xx in range(2):
+        p = project(xx, slice(0, 256))
+        qr[xx] = p[:, :128].reshape(4, 128, 128)
+        mixed[0, xx] = p[:, 128:]
+        p = project(xx, slice(256, 512))
+        kr[xx] = p[:, :128].reshape(4, 128, 128)
+        vv[xx] = p[:, 128:].astype(BF16).reshape(4, 128, 128)
+        mixed[1, xx] = project(xx, slice(512, 640))
+    x0, x1 = mixed[0, 0], mixed[0, 1]
+    qr[2] = jnp.where(low_head, x0, pltpu.roll(x1, 64, 1)).reshape(4, 128, 128)
+    kr[2] = jnp.where(low_head, pltpu.roll(x0, 64, 1), x1).reshape(4, 128, 128)
+    x0, x1 = mixed[1, 0], mixed[1, 1]
+    vv[2] = jnp.where(low_head, x0, pltpu.roll(x1, 64, 1)).astype(BF16).reshape(4, 128, 128)
+    gc.step5()
+    gf.step3()
+    block = head_block()
+    cos = cos_ref[...].reshape(512, 128)
+    sin = sin_ref[...].reshape(512, 128)
+
+    def turned(raw, gain):
+        raw = raw.reshape(512, 128)
+        v = raw * lax.rsqrt(head_mean(raw * raw, block) + EPSILON) * gain
+        return v * cos + swap_quarters(v) * sin
+
+    for p in range(3):
+        q = turned(qr[p], hg_ref[0:1, :]).astype(BF16)
+        q8[p] = (q.astype(F32) * 0.125).astype(BF16).reshape(4, 128, 128)
+        kk[p] = turned(kr[p], hg_ref[1:2, :]).astype(BF16).reshape(4, 128, 128)
+    load_cap.wait()
+    gc.finish()
+    text_acc[...] = jnp.zeros((2, 256, 384), F32)
+
+    def text_step(i, carry):
+        xx = i // 8
+        j = i % 8
+        w_cols = w_c[xx, j // 4, j % 4].reshape(512, 384)
+        text_acc[xx] += mm(cap[:, tile(j, 512)], w_cols)
+        return carry
+
+    lax.fori_loop(0, 16, text_step, 0)
+    gf.step4()
+    low_text = lanes((256, 128)) < 64
+    for xx in range(2):
+        tkr[xx] = text_acc[xx, :, 0:128]
+        tv[xx] = text_acc[xx, :, 256:384].astype(BF16)
+    x0, x1 = text_acc[0, :, 128:256], text_acc[1, :, 128:256]
+    tkr[2] = jnp.where(low_text, x0, pltpu.roll(x1, 64, 1))
+    tv[2] = jnp.where(low_text, pltpu.roll(x0, 64, 1), x1).astype(BF16)
+    for p in range(3):
+        raw = tkr[p]
+        tk[p] = (raw * lax.rsqrt(head_mean(raw * raw, block) + EPSILON) * hg_ref[2:3, :]).astype(BF16)
+
+    self_bias = key_bias(512, z, length)
+    text_bias = key_bias(256, z, text_len)
+    lse_ref[...] = jnp.zeros((4, 128, 128), F32)
+
+    def attend(p):
+        def rows_step(b, carry):
+            slots = pl.ds(b * 2, 2)
+            q = q8[p, slots].reshape(256, 128)
+            low_rows = lanes((256, 128)) < 64
+            own = jnp.zeros((256, 128), F32)
+            other = jnp.zeros((256, 128), F32)
+            for head in range(2):
+                keep = low_rows if head == 0 else jnp.logical_not(low_rows)
+                qm = jnp.where(keep, q, jnp.zeros_like(q))
+                for text in range(2):
+                    k = tk[p] if text else kk[p].reshape(512, 128)
+                    v = tv[p] if text else vv[p].reshape(512, 128)
+                    scores = mm_t(qm, k) + (text_bias if text else self_bias)
+                    top = jnp.max(scores, axis=-1, keepdims=True)
+                    e = jnp.exp(scores - top)
+                    total = jnp.sum(e, axis=-1, keepdims=True)
+                    probs = (e * (1.0 / total)).astype(BF16)
+                    mix = jnp.where(keep, mm(probs, v), 0.0)
+                    lane = p * 2 + head + 8 * text
+                    lse_ref[slots, :, lane : lane + 1] = (top + jnp.log(total)).reshape(2, 128, 1)
+                    if text:
+                        other = other + mix
+                    else:
+                        own = own + mix
+            other_ref[p, slots] = other.reshape(2, 128, 128)
+            both = own + gate_ref[p : p + 1, :] * other
+            if p < 2:
+                cw[p, slots, :, 128:256] = both.astype(BF16).reshape(2, 128, 128)
+            else:
+                moved = pltpu.roll(both, 64, 1)
+                zero = jnp.zeros_like(both)
+                cw[0, slots, :, 0:128] = jnp.where(low_rows, zero, moved).astype(BF16).reshape(2, 128, 128)
+                cw[1, slots, :, 0:128] = jnp.where(low_rows, zero, both).astype(BF16).reshape(2, 128, 128)
+            return carry
+
+        lax.fori_loop(0, 2, rows_step, 0)
+
+    attend(0)
+    gf.step5()
+    attend(1)
+    attend(2)
+
+    def out_rows(lo, count):
+        n = count * 128
+        a0 = cw[0, lo : lo + count].reshape(n, 256)
+        a1 = cw[1, lo : lo + count].reshape(n, 256)
+        for xb in range(2):
+            cols = slice(xb * 768, xb * 768 + 768)
+            b0 = w_a[0, xb, :, :, :, 512:768].reshape(768, 256)
+            b1 = w_a[1, xb, :, :, :, 512:768].reshape(768, 256)
+            total = mm_t(a0, b0) + mm_t(a1, b1)
+            part[lo : lo + count, :, cols] = total.astype(BF16).reshape(count, 128, 768)
+
+    sums = ZScatter(send, part, relay, got, right, left)
+    out_rows(1, 2)
+    sums.near()
+    out_rows(3, 1)
+    sums.far()
+    out_rows(0, 1)
+    sums.pass_on()
+    attn = sums.total()
+    attn_ref[...] = attn
+    unit_two, _ = normalize(attn)
+    live = live_ref[...][:, :1]
+    middle = resid_ref[...].astype(F32) + live * jnp.tanh(mod_ref[1:2, :]) * unit_two * gains_ref[1:2, :]
+    mid_ref[...] = middle
+    unit_three, _ = normalize(middle)
+    second_ref[...] = (unit_three * gains_ref[2:3, :] * (1.0 + mod_ref[2:3, :])).astype(BF16)
+    cot_swap.wait_recv()
+    gf.finish()
+    send.drain()
+
+
+def attention_call(args, cid):
+    S = jax.ShapeDtypeStruct
+    vm = pl.BlockSpec(memory_space=VMEM)
+    sm = pl.BlockSpec(memory_space=pltpu.SMEM)
+    any_ = pl.BlockSpec(memory_space=pl.ANY)
+    pair = (3, 4, 128, 128)
+    outs = [
+        S((2, 2, 4, 2, 96, 768), BF16),
+        S((2, 2, 4, 2, 96, D), BF16),
+        S((4, 128, D), BF16),
+        S((128, D), BF16),
+        S((2, 64, D), BF16),
+        S(pair, BF16),
+        S(pair, BF16),
+        S(pair, BF16),
+        S(pair, F32),
+        S(pair, F32),
+        S((3, 256, 128), BF16),
+        S((3, 256, 128), BF16),
+        S((3, 256, 128), F32),
+        S(pair, F32),
+        S((4, 128, 128), F32),
+        S((2, 4, 128, 256), BF16),
+        S((128, D), F32),
+        S((128, D), F32),
+        S((128, D), BF16),
+        S((8, D), F32),
+        S((8, D), F32),
+        S((16, 8, 128), F32),
+        S((4, 128, 128), F32),
+        S((4, 128, 128), F32),
+        S((128, 128), F32),
+    ]
+    return pl.pallas_call(
+        attention_kernel,
+        out_shape=outs,
+        in_specs=[vm] * 11 + [any_] + [vm] * 2 + [sm] * 4,
+        out_specs=[vm, any_] + [vm] * (len(outs) - 2),
+        scratch_shapes=[
+            VMEM((96, 768), BF16),
+            VMEM((96, D), BF16),
+            VMEM((256, 384), BF16),
+            VMEM((2, 2, 4, 2, 256, 384), BF16),
+            VMEM((256, 4096), BF16),
+            VMEM((4, 2, 64, D), BF16),
+            VMEM((2, 64, D), BF16),
+            VMEM((16, 8, 128), F32),
+            VMEM((16, 16, 128), F32),
+            VMEM((16, 16, 128), F32),
+            VMEM((8, 16, 128), F32),
+            VMEM((2, 2, 512, 128), F32),
+            VMEM((2, 256, 384), F32),
+            VMEM((4, 128, D), BF16),
+            VMEM((2, 64, D), BF16),
+            VMEM((2, 128, D), BF16),
+            pltpu.SemaphoreType.DMA((4,)),
+        ]
+        + dma_sems(160),
+        compiler_params=pltpu.CompilerParams(
+            collective_id=cid, has_side_effects=True, vmem_limit_bytes=56 * 2**20
+        ),
+        name="attention",
+    )(*args)
+
+
+def ffn_kernel(
+    x_ref,
+    w_hbm,
+    mid_ref,
+    attn_ref,
+    cot_ref,
+    mod_ref,
+    gain_ref,
+    live_ref,
+    out_ref,
+    gmid_ref,
+    gattn_ref,
+    sums_ref,
+    dw_ref,
+    w,
+    x_all,
+    g_all,
+    act,
+    dgate,
+    dup,
+    gpre,
+    part1,
+    part2,
+    relay1,
+    relay2,
+    got1,
+    got2,
+    flip,
+    own_g,
+    w_sem,
+    ss,
+    rs,
+):
+    z, right, left = z_ring()
+    load = pltpu.make_async_copy(w_hbm, w, w_sem)
+    load.start()
+    greet([right, left])
+    send = Sender(ss, rs)
+    one = ZGather(send, x_ref, x_all, right, left)
+    x_all[0] = x_ref[...]
+    load.wait()
+
+    def pre(lo, count):
+        rows = count * 128
+        x = x_all[lo : lo + count].reshape(rows, D)
+        for xx in range(2):
+
+            def column(j, carry, xx=xx):
+                g = mm(x, w[xx, :, tile(j)])
+                u = mm(x, w[xx, :, tile(j + 2)])
+                s = jax.nn.sigmoid(g)
+                gs = g * s
+                act[xx, lo : lo + count, :, tile(j)] = (gs * u).astype(BF16).reshape(count, 128, 256)
+                dgate[xx, lo : lo + count, :, tile(j)] = (u * s * (1.0 + g * (1.0 - s))).reshape(count, 128, 256)
+                dup[xx, lo : lo + count, :, tile(j)] = gs.reshape(count, 128, 256)
+                return carry
+
+            lax.fori_loop(0, 2, column, 0)
+
+    def down(lo, count):
+        rows = count * 128
+        a0 = act[0, lo : lo + count].reshape(rows, 512)
+        a1 = act[1, lo : lo + count].reshape(rows, 512)
+
+        def column(j, carry):
+            cols = tile(j)
+            total = mm_t(a0, w[0, cols, 1024:1536]) + mm_t(a1, w[1, cols, 1024:1536])
+            part1[lo : lo + count, :, cols] = total.astype(BF16).reshape(count, 128, 256)
+            return carry
+
+        lax.fori_loop(0, D // 256, column, 0)
+
+    sum1 = ZScatter(send, part1, relay1, got1, right, left)
+    pre(0, 1)
+    one.near()
+    pre(1, 2)
+    down(1, 2)
+    sum1.near()
+    one.far()
+    pre(3, 1)
+    down(3, 1)
+    sum1.far()
+    down(0, 1)
+    transpose_into(x_all, flip)
+    sum1.pass_on()
+    ffn_total = sum1.total()
+
+    live = live_ref[...][:, :1]
+    mod = mod_ref[...]
+    gains = gain_ref[...]
+    gate_f = jnp.tanh(mod[3:4])
+    middle = mid_ref[...]
+    unit_four, inverse_four = normalize(ffn_total)
+    out_ref[...] = (middle + live * gate_f * unit_four * gains[3:4]).astype(BF16)
+    grad_top = cot_ref[...].astype(F32)
+    weighted = grad_top * live
+    part_four = jnp.sum(weighted * unit_four, axis=0, keepdims=True)
+    own_g[...] = norm_back(unit_four, inverse_four, weighted * gate_f * gains[3:4]).astype(BF16)
+    two = ZGather(send, own_g, g_all, right, left)
+    g_all[0] = own_g[...]
+    sums_ref[3:4, :] = part_four * gains[3:4] * (1.0 - gate_f * gate_f)
+    sums_ref[7:8, :] = part_four * gate_f
+
+    def back(lo, count):
+        rows = count * 128
+        g = g_all[lo : lo + count].reshape(rows, D)
+        for xx in range(2):
+
+            def column(j, carry, xx=xx):
+                ga = mm(g, w[xx, :, tile(j + 4)])
+                dg = dgate[xx, lo : lo + count, :, tile(j)].reshape(rows, 256)
+                du = dup[xx, lo : lo + count, :, tile(j)].reshape(rows, 256)
+                gpre[xx, lo : lo + count, :, tile(j)] = (ga * dg).astype(BF16).reshape(count, 128, 256)
+                gpre[xx, lo : lo + count, :, tile(j + 2)] = (ga * du).astype(BF16).reshape(count, 128, 256)
+                return carry
+
+            lax.fori_loop(0, 2, column, 0)
+
+    def back_in(lo, count):
+        rows = count * 128
+        a0 = gpre[0, lo : lo + count].reshape(rows, 1024)
+        a1 = gpre[1, lo : lo + count].reshape(rows, 1024)
+
+        def column(j, carry):
+            cols = tile(j)
+            total = mm_t(a0, w[0, cols, 0:1024]) + mm_t(a1, w[1, cols, 0:1024])
+            part2[lo : lo + count, :, cols] = total.astype(BF16).reshape(count, 128, 256)
+            return carry
+
+        lax.fori_loop(0, D // 256, column, 0)
+
+    sum2 = ZScatter(send, part2, relay2, got2, right, left)
+    back(0, 1)
+    two.near()
+    back(1, 2)
+    back_in(1, 2)
+    sum2.near()
+    two.far()
+    back(3, 1)
+    back_in(3, 1)
+    sum2.far()
+    back_in(0, 1)
+
+    def weight_grad(right_of, first, count):
+        def column(i, carry):
+            xx = i // count
+            j = i % count
+            b = right_of(xx, j).reshape(512, 256)
+            for r in range(0, D, 512):
+                dw_ref[xx, r : r + 512, tile(j + first)] = mm(flip[r : r + 512, :], b).astype(BF16)
+            return carry
+
+        lax.fori_loop(0, 2 * count, column, 0)
+
+    weight_grad(lambda xx, j: gpre[xx, :, :, tile(j)], 0, 4)
+    sum2.pass_on()
+    transpose_into(g_all, flip)
+    weight_grad(lambda xx, j: act[xx, :, :, tile(j)], 4, 2)
+    grad_second = sum2.total()
+
+    scale_f = mod[2:3]
+    unit_three, inverse_three = normalize(middle)
+    sum_three = jnp.sum(grad_second * unit_three, axis=0, keepdims=True)
+    sums_ref[2:3, :] = sum_three * gains[2:3]
+    sums_ref[6:7, :] = sum_three * (1.0 + scale_f)
+    grad_middle = grad_top + norm_back(
+        unit_three, inverse_three, grad_second * (1.0 + scale_f) * gains[2:3]
+    )
+    gmid_ref[...] = grad_middle
+    gate_a = jnp.tanh(mod[1:2])
+    unit_two, inverse_two = normalize(attn_ref[...])
+    weighted_mid = grad_middle * live
+    sum_two = jnp.sum(weighted_mid * unit_two, axis=0, keepdims=True)
+    sums_ref[1:2, :] = sum_two * gains[1:2] * (1.0 - gate_a * gate_a)
+    sums_ref[5:6, :] = sum_two * gate_a
+    sums_ref[0:1, :] = jnp.zeros((1, D), F32)
+    sums_ref[4:5, :] = jnp.zeros((1, D), F32)
+    gattn_ref[...] = norm_back(unit_two, inverse_two, weighted_mid * gate_a * gains[1:2]).astype(BF16)
+    send.drain()
+
+
+def ffn_call(second_in, w_f, middle, attn, cot, mod_rows, gains, live, cid):
+    S = jax.ShapeDtypeStruct
+    vm = pl.BlockSpec(memory_space=VMEM)
+    any_ = pl.BlockSpec(memory_space=pl.ANY)
+    return pl.pallas_call(
+        ffn_kernel,
+        out_shape=[
+            S((128, D), BF16),
+            S((128, D), F32),
+            S((128, D), BF16),
+            S((8, D), F32),
+            S((2, D, D), BF16),
+        ],
+        in_specs=[vm, any_] + [vm] * 6,
+        out_specs=[vm] * 5,
+        scratch_shapes=[
+            VMEM((2, D, D), BF16),
+            VMEM((4, 128, D), BF16),
+            VMEM((4, 128, D), BF16),
+            VMEM((2, 4, 128, 512), BF16),
+            VMEM((2, 4, 128, 512), F32),
+            VMEM((2, 4, 128, 512), F32),
+            VMEM((2, 4, 128, 1024), BF16),
+            VMEM((4, 128, D), BF16),
+            VMEM((4, 128, D), BF16),
+            VMEM((2, 64, D), BF16),
+            VMEM((2, 64, D), BF16),
+            VMEM((2, 128, D), BF16),
+            VMEM((2, 128, D), BF16),
+            VMEM((D, 512), BF16),
+            VMEM((128, D), BF16),
+            pltpu.SemaphoreType.DMA,
+        ]
+        + dma_sems(20),
+        compiler_params=pltpu.CompilerParams(
+            collective_id=cid, has_side_effects=True, vmem_limit_bytes=56 * 2**20
+        ),
+        name="ffn",
+    )(second_in, w_f, middle, attn, cot, mod_rows, gains, live)
+
+
 def pick(array, index):
     return lax.dynamic_index_in_dim(array, index, 0, keepdims=False)
 
@@ -576,146 +1423,128 @@
     t = lax.axis_index("tensor")
     z = t // 2
     xl = t % 2
-    scaling = HD ** (-0.5)
-    d_shard = jnp.concatenate(
+    def head_tiles(rows):
+        return jnp.concatenate([rows, rows], axis=-1)
+
+    head_scales = head_gains.astype(F32)
+    hg2 = jnp.pad(head_tiles(head_scales), ((0, 5), (0, 0)))
+    gate_values = jnp.tanh(lax.dynamic_slice_in_dim(head_gate.astype(F32), z * 6, 6, 0))
+    gate_tile = jnp.pad(
+        jnp.repeat(gate_values[jnp.array([0, 1, 3, 4, 2, 5])].reshape(3, 2), 64, axis=1),
+        ((0, 5), (0, 0)),
+    )
+    (
+        w_a,
+        w_f,
+        first_rel,
+        resid_b,
+        cot,
+        q8,
+        kk,
+        vv,
+        qr,
+        kr,
+        tk,
+        tv,
+        tkr,
+        other_rel,
+        lse,
+        cw,
+        attn,
+        middle,
+        second_in,
+        mod8,
+        gains8,
+        got1,
+        cos_t,
+        sin_t,
+        live128,
+    ) = attention_call(
         [
-            qkv_weight[0],
-            qkv_weight[1],
-            qkv_weight[2],
+            hidden[:, 0],
+            cotangent[:, 0],
+            condition[:, 0],
+            norm_gains,
+            ada_bias[None],
+            ada_weight,
+            qkv_weight,
             out_weight.T,
-            ffn_weight[0],
-            ffn_weight[1],
+            ffn_weight,
             down_weight.T,
+            caption_weight,
+            caption[:, 0],
+            hg2,
+            gate_tile,
+            lengths,
+            frames,
+            widths,
+            caption_lens,
         ],
-        axis=1,
-    )
-    c_shard = jnp.concatenate([caption_weight[0], caption_weight[1]], axis=1)
-    unit_rows = swish(condition[:, 0].astype(F32)).astype(BF16)
-    unit_msg = jnp.transpose(unit_rows.astype(F32).reshape(2, 16, 64), (1, 0, 2))
-    unit_msg = jnp.pad(unit_msg, ((0, 0), (0, 2), (0, 64)))
-    gain_msg = jnp.broadcast_to(jnp.pad(norm_gains.astype(F32), ((0, 0), (0, 32)))[None], (16, 4, 128))
-    msg = jnp.concatenate([unit_msg, gain_msg], axis=1)
-    ada_pad = jnp.pad(ada_weight, ((0, 64), (0, 0)))
-    bias_f = ada_bias.astype(F32)
-    bias_row = jnp.where(
-        t == dp // 2,
-        jnp.where(
-            dp % 2 == 0,
-            jnp.concatenate([bias_f, jnp.zeros((384,), F32)]),
-            jnp.concatenate([jnp.zeros((384,), F32), bias_f]),
-        ),
-        0.0,
-    )[None]
-    got1, got3 = kernel_call(
-        mod_kernel,
-        [msg, ada_pad, bias_row],
-        [S((16, 8, 128), F32), S((8, 8, 768), F32)],
         1,
-        [VMEM((16, 8, 768), F32), VMEM((16, 8, 768), F32)]
-        + dma_sems(15)
-        + dma_sems(15)
-        + dma_sems(7),
-        name="modulation",
-    )
+    )
+    w_f = w_f.reshape(2, D, D)
+    w_a = w_a.reshape(2, D, 768)
+    perm = jnp.array([0, 2, 3, 1])[(jnp.arange(4) - z) % 4]
+
+    def nat(v):
+        return v[perm].reshape((512,) + v.shape[2:])
+
+    def heads_of(v):
+        v = jnp.stack([nat(v[i]) for i in range(3)]) if v.ndim == 4 else v
+        v = v.reshape(3, v.shape[1], 2, 64)
+        return jnp.stack([v[0, :, 0], v[0, :, 1], v[2, :, 0], v[1, :, 0], v[1, :, 1], v[2, :, 1]], axis=1)
+
+    mod_rows, gains = mod8[:4], gains8[:4]
+    scale_attn = mod_rows[0]
     units = got1[:, 0:2, :64].reshape(32, 64)
-    gains = jnp.transpose(got1[:, 4:8, :96], (1, 0, 2)).reshape(4, D)
-    mod_rows = jnp.where(xl == 0, got3[:, 0], got3[:, 1]).reshape(4, D)
-    scale_attn, gate_attn, scale_ffn, gate_ffn = (mod_rows[i] for i in range(4))
-    hid_all, cot = kernel_call(
-        hidden_kernel,
-        [hidden[:, 0], cotangent[:, 0]],
-        [S((4, 2, 64, D), BF16), S((2, 64, D), BF16)],
-        2,
-        dma_sems(6),
-        name="hidden_gather",
-    )
-    resid = pick(hid_all, z).reshape(128, D).astype(F32)
-    grad_top = cot.reshape(128, D).astype(F32)
-    w_d = plane_gather(d_shard, 3)
-    w_c = plane_gather(c_shard, 4)
-
+    first_all = nat(first_rel)
+    resid = resid_b.astype(F32)
+    w_q = w_a[:, :, :192]
+    w_k = jnp.concatenate([w_a[:, :, 256:384], w_a[:, :, 192:256]], axis=2)
+    w_v = w_a[:, :, 384:576]
+    w_o = jnp.concatenate([w_a[:, :, 640:768], w_a[:, :, 576:640]], axis=2)
+    unit_one, inverse_one = normalize(resid)
+    query_unit, query_inverse = normalize(heads_of(qr))
+    key_unit, key_inverse = normalize(heads_of(kr))
+    text_unit, text_inverse = normalize(heads_of(tkr))
+    queries, keys, values = heads_of(q8) * 8.0, heads_of(kk), heads_of(vv)
+    text_keys, text_values = heads_of(tk), heads_of(tv)
+    other = heads_of(other_rel)
+    cos64, sin64 = nat(cos_t), nat(sin_t)
+    cosine, sine_table = cos64[:, :32], -sin64[:, :32]
+    lse_n = nat(lse)
+    horder = jnp.array([0, 1, 4, 2, 3, 5])
     length = pick(lengths[:, 0], xl)
-    frame_count = pick(frames[:, 0], xl)
-    width = pick(widths[:, 0], xl)
     text_len = pick(caption_lens[:, 0], xl)
     cap = pick(caption[:, 0], xl)
-    slot_rows = z * 128 + jnp.arange(128, dtype=jnp.int32)
-    live_rows = (slot_rows < length).astype(F32)[:, None]
-    key_live = jnp.arange(512, dtype=jnp.int32) < length
-    text_live = jnp.arange(256, dtype=jnp.int32) < text_len
-    cosine, sine_table = rope_tables(length, frame_count, width, 512, HD)
-    head_scales = head_gains.astype(F32)
-    gate_values = jnp.tanh(lax.dynamic_slice_in_dim(head_gate.astype(F32), z * 6, 6, 0))
-
-    unit_all, _ = normalize(hid_all.reshape(512, D).astype(F32))
-    first_all = (unit_all * gains[0] * (1.0 + scale_attn)).astype(BF16)
-    unit_one, inverse_one = normalize(resid)
-    w_q, w_k, w_v, w_o = (w_d[:, :, i * 192 : (i + 1) * 192] for i in range(4))
-    w_g, w_u, w_dn = (w_d[:, :, 768 + i * 512 : 768 + (i + 1) * 512] for i in range(3))
-    w_ck, w_cv = w_c[:, :, :192], w_c[:, :, 192:]
+    key_live = jnp.arange(512) < length
+    text_live = jnp.arange(256) < text_len
+    scaling = 0.125
+
+    def reprob(keyset, live, lses):
+        sc = dot("qhd,khd->hqk", queries, keyset) * scaling
+        sc = jnp.where(live[None, None], sc, NEGATIVE)
+        return jnp.exp(sc - lses.T[:, :, None])
+
+    probs = reprob(keys, key_live, lse_n[:, :6][:, horder])
+    text_probs = reprob(text_keys, text_live, lse_n[:, 8:14][:, horder])
+    comb0 = jnp.concatenate([nat(cw[0])[:, 128:256], nat(cw[0])[:, 64:128]], axis=1)
+    comb1 = jnp.concatenate([nat(cw[1])[:, 128:256], nat(cw[1])[:, 64:128]], axis=1)
+    combined = jnp.stack([comb0, comb1], axis=1)
     hs = (512, 6, HD)
     ts = (256, 6, HD)
-    q_raw, k_raw, v_raw = (dot("sd,xdk->sxk", first_all, w).reshape(hs) for w in (w_q, w_k, w_v))
-    query_unit, query_inverse = normalize(q_raw)
-    key_unit, key_inverse = normalize(k_raw)
-    queries = rotate(query_unit * head_scales[0], cosine, sine_table).astype(BF16)
-    keys = rotate(key_unit * head_scales[1], cosine, sine_table).astype(BF16)
-    values = v_raw.astype(BF16)
-    text_raw = dot("td,xdk->txk", cap, w_ck).reshape(ts)
-    text_unit, text_inverse = normalize(text_raw)
-    text_keys = (text_unit * head_scales[2]).astype(BF16)
-    text_values = dot("td,xdk->txk", cap, w_cv).reshape(ts).astype(BF16)
-
-    def softmax(scores, live):
-        masked = jnp.where(live[None, None, :], scores, NEGATIVE)
-        top = jnp.max(masked, axis=-1, keepdims=True)
-        e = jnp.exp(masked - top)
-        return e / jnp.sum(e, axis=-1, keepdims=True)
-
-    probs = softmax(dot("qhd,khd->hqk", queries, keys) * scaling, key_live)
-    own = dot("hqk,khd->qhd", probs.astype(BF16), values)
-    text_probs = softmax(dot("qhd,khd->hqk", queries, text_keys) * scaling, text_live)
-    other = dot("hqk,khd->qhd", text_probs.astype(BF16), text_values)
-    combined = (own + gate_values[None, :, None] * other).astype(BF16).reshape(512, 2, 192)
-    attn = z_scatter(dot("sxk,xdk->sd", combined, w_o).astype(BF16), 5)
-    unit_two, inverse_two = normalize(attn)
-    gate_a = jnp.tanh(gate_attn)
-    middle = resid + live_rows * gate_a * unit_two * gains[1]
-    unit_three, inverse_three = normalize(middle)
-    second_in = (unit_three * gains[2] * (1.0 + scale_ffn)).astype(BF16)
-    second_all = z_gather(second_in, 6)
-    pre_g = dot("sd,xdf->sxf", second_all, w_g)
-    pre_u = dot("sd,xdf->sxf", second_all, w_u)
-    sigma = jax.nn.sigmoid(pre_g)
-    activated = (pre_g * sigma * pre_u).astype(BF16)
-    ffn_total = z_scatter(dot("sxf,xdf->sd", activated, w_dn).astype(BF16), 7)
-    unit_four, inverse_four = normalize(ffn_total)
-    gate_f = jnp.tanh(gate_ffn)
-    layer_out = (middle + live_rows * gate_f * unit_four * gains[3]).astype(BF16)
-
-    weighted = grad_top * live_rows
-    gain_four = jnp.sum(weighted * gate_f * unit_four, axis=0)
-    gate_ffn_grad = jnp.sum(weighted * unit_four * gains[3], axis=0) * (1.0 - gate_f * gate_f)
-    grad_ffn_in = norm_back(unit_four, inverse_four, weighted * gate_f * gains[3]).astype(BF16)
-    grad_two = z_gather(grad_ffn_in, 8)
-    grad_act = dot("sd,xdf->sxf", grad_two, w_dn)
-    down_grad = dot("sd,sxf->xdf", grad_two, activated)
-    grad_g = (grad_act * pre_u * sigma * (1.0 + pre_g * (1.0 - sigma))).astype(BF16)
-    grad_u = (grad_act * pre_g * sigma).astype(BF16)
-    gate_grad = dot("sd,sxf->xdf", second_all, grad_g)
-    up_grad = dot("sd,sxf->xdf", second_all, grad_u)
-    grad_second = z_scatter(
-        (dot("sxf,xdf->sd", grad_g, w_g) + dot("sxf,xdf->sd", grad_u, w_u)).astype(BF16), 9
-    )
-    scale_ffn_grad = jnp.sum(grad_second * unit_three * gains[2], axis=0)
-    gain_three = jnp.sum(grad_second * (1.0 + scale_ffn) * unit_three, axis=0)
-    grad_middle = grad_top + norm_back(
-        unit_three, inverse_three, grad_second * (1.0 + scale_ffn) * gains[2]
-    )
-    weighted_mid = grad_middle * live_rows
-    gain_two = jnp.sum(weighted_mid * gate_a * unit_two, axis=0)
-    gate_attn_grad = jnp.sum(weighted_mid * unit_two * gains[1], axis=0) * (1.0 - gate_a * gate_a)
-    grad_attn_in = norm_back(unit_two, inverse_two, weighted_mid * gate_a * gains[1]).astype(BF16)
+    layer_out, grad_middle, grad_attn_in, ffn_sums, f_grad = ffn_call(
+        second_in,
+        w_f,
+        middle,
+        attn,
+        cot.reshape(128, D),
+        mod8,
+        gains8,
+        live128,
+        6,
+    )
+    grad_top = cot.reshape(128, D).astype(F32)
     grad_one = z_gather(grad_attn_in, 10)
     grad_combined = dot("sd,xdk->sxk", grad_one, w_o).astype(BF16)
     out_grad = dot("sd,sxk->xdk", grad_one, combined)
@@ -771,9 +1600,6 @@
             dot("sd,sxk->xdk", first_all, grad_k).astype(BF16),
             dot("sd,sxk->xdk", first_all, grad_v).astype(BF16),
             out_grad.astype(BF16),
-            gate_grad.astype(BF16),
-            up_grad.astype(BF16),
-            down_grad.astype(BF16),
         ],
         axis=2,
     )
@@ -785,6 +1611,7 @@
         axis=2,
     )
     d_out = plane_scatter(d_grad, 12)
+    f_out = plane_scatter(f_grad, 17)
     c_out = plane_scatter(c_grad, 13)
     out_half = layer_out.reshape(2, 64, D)
     grad_half = grad_hidden.reshape(2, 64, D)
@@ -800,9 +1627,9 @@
     layer_final = jnp.where(mine, pick(out_half, xl)[None], pick(out_got, 1 - xl)[None])
     grad_final = jnp.where(mine, pick(grad_half, xl)[None], pick(grad_got, 1 - xl)[None])
 
-    mod_grad = jnp.stack([scale_attn_grad, gate_attn_grad, scale_ffn_grad, gate_ffn_grad])
+    mod_grad = jnp.concatenate([scale_attn_grad[None], ffn_sums[1:4]])
     mod_msg = jnp.pad(mod_grad.reshape(8, 6, 128), ((0, 0), (0, 2), (0, 0)))
-    gain_grad = jnp.stack([gain_one, gain_two, gain_three, gain_four])
+    gain_grad = jnp.concatenate([gain_one[None], ffn_sums[5:8]])
     gain_part = jnp.pad(
         jnp.transpose(gain_grad.reshape(4, 16, 96), (1, 0, 2)), ((0, 0), (0, 0), (0, 32))
     )
@@ -839,8 +1666,8 @@
         jnp.stack([c_out[:, :192], c_out[:, 192:]]),
         heads[192:216],
         d_out[:, 576:768].T,
-        jnp.stack([d_out[:, 768:1280], d_out[:, 1280:1792]]),
-        d_out[:, 1792:].T,
+        jnp.stack([f_out[:, :512], f_out[:, 512:1024]]),
+        f_out[:, 1024:].T,
     )
 
 

time: 707 us -> 565 us (0.80)
  matrix products: 112 us -> 37.3 us
  other arithmetic: 71.7 us -> 30.9 us
  Pallas kernels: 408 us -> 371 us
  local copies, waits for them, and re-layouts: 101 us -> 113 us
    pallas_call x15 -> x7, Pallas kernels: 408 us -> 197 us  [kernel_call(): pl.pallas_call(body, out_shape=out_shape, in_specs=[pl.BlockSpec(memory_s...]
    pallas_call x0 -> x2, Pallas kernels: none -> 174 us  [the longest x1 107 us: attention_call(): pl.pallas_call(attention_kernel, out_shape=outs, in_specs=[vm] * 11 + [an...]
    dot_general x34 -> x19, matrix products: 97.6 us -> 33.1 us  [dot(): return jnp.einsum(spec, a, b, preferred_element_type=F32)]
    gather x0 -> x46, local copies, waits for them, and re-layouts: none -> 22.6 us  [the longest x42 18.9 us: nat(): return v[perm].reshape((512,) + v.shape[2:])]
    dot_general x6 -> x0, local copies, waits for them, and re-layouts: 22.1 us -> none  [dot(): return jnp.einsum(spec, a, b, preferred_element_type=F32)]
    unnamed x197 -> x171, local copies, waits for them, and re-layouts: 17 us -> 34.3 us
    reduce_sum x3 -> x0, other arithmetic: 17.2 us -> none  [the longest x1 11.7 us: on_device(): gain_four = jnp.sum(weighted * gate_f * unit_four, axis=0)]
    concatenate x1, local copies, waits for them, and re-layouts: 17.5 us -> 6.81 us  [on_device(): jnp.concatenate([dot('sd,sxk->xdk', first_all, grad_q).astype(BF16), dot(...]
where the time goes in v2:
time: 565 us; the launch traced here: 554 us
  Pallas kernels  371 us (66%)
  local copies, waits for them, and re-layouts  113 us (20%)
  matrix products  37.3 us (7%)
  other arithmetic  30.9 us (5%)
    pallas_call x7, Pallas kernels, kernel_call(): pl.pallas_call(body, out_shape=out_shape, in_specs=[pl.BlockSpec(memory_s...  197 us
    pallas_call x1, Pallas kernels, attention_call(): pl.pallas_call(attention_kernel, out_shape=outs, in_specs=[vm] * 11 + [an...  107 us
    pallas_call x1, Pallas kernels, ffn_call(): pl.pallas_call(ffn_kernel, out_shape=[S((128, D), BF16), S((128, D), F32)...  67.1 us
    unnamed x171, local copies, waits for them, and re-layouts  34.3 us
    dot_general x19, matrix products, dot(): return jnp.einsum(spec, a, b, preferred_element_type=F32)  33.1 us
    gather x42, local copies, waits for them, and re-layouts, nat(): return v[perm].reshape((512,) + v.shape[2:])  18.9 us

profile of v2, /device:TPU:1, one launch (start us, length us, event | category | flops | bytes accessed | tf_op | source)
XLA Modules:
  0.0 554.2 jit_solution(7465191384883812495)
XLA Ops:
  21.6 107.1 %attention.1 = (bf16[2,2,4,2,96,768]{5,4,3,2,1,0:T(8,128)(2,1)}, bf16[2,2,4,2,96,1536]{5,4,3,2,1,0:T(8,128)(2,1)}, bf16[4,128,1536]{2,1,0:T(8,128)(2,1)}, bf16[1...) custom-call(bf16[2,64,1536]{2,1,0:T(8,128)(2,1)} %bitcast.584, ...), custom_call_target="tpu_custom_call" | custom-call | tf_op jit(solution)/shard_map/attention/pallas_call | solution.py:1139
  128.7 67.1 %ffn.1 = (bf16[128,1536]{1,0:T(8,128)(2,1)}, f32[128,1536]{1,0:T(8,128)}, bf16[128,1536]{1,0:T(8,128)(2,1)}, f32[8,1536]{1,0:T(8,128)}, bf16[2,1536,1536]{2,1,0:T(8,128)(2,1)}) custom-call(bf16[128,1536]{1,0:T(8,128)(2,1)} %get-tuple-element.47.x_ref, bf16[2,1536,1536]{2,1,0:T(8,128)(2,1)} %bitcast.528, f32[128,1536]{1,0:T(8,128)} %get-tuple-element.49.mid_ref, ...), custom_call_target="tpu_custom_call" | custom-call | tf_op jit(solution)/shard_map/ffn/pallas_call | solution.py:1356
  237.0 58.0 %plane_scatter17.1 = f32[96,1536]{1,0:T(8,128)} custom-call(bf16[2,2,4,2,96,1536]{5,4,3,2,1,0:T(8,128)(2,1)} %bitcast.527), custom_call_target="tpu_custom_call" | custom-call | tf_op jit(solution)/shard_map/plane_scatter17/pallas_call | solution.py:70
  310.6 3.2 gather_fusion.25
  316.0 17.1 %z_gather10.1 = bf16[4,128,1536]{2,1,0:T(8,128)(2,1)} custom-call(bf16[128,1536]{1,0:T(8,128)(2,1)} %get-tuple-element.62.x_ref), custom_call_target="tpu_custom_call" | custom-call | tf_op jit(solution)/shard_map/z_gather10/pallas_call | solution.py:70
  333.1 3.4 fusion.12
  336.5 2.7 fusion.106
  339.2 2.1 copy.233
  341.7 2.4 fusion.105
  344.0 2.3 copy.232
  348.8 2.3 fusion.109
  353.6 2.1 multiply_reduce_fusion.1
  361.0 3.4 pad_maximum_fusion
  364.4 8.8 %copy.218 = bf16[2,4096,384]{2,1,0:T(8,128)(2,1)} copy(bf16[2,4096,384]{1,2,0:T(8,128)(2,1)} %pad_maximum_fusion) | data formatting | bytes 12582912 | tf_op jit(solution)/shard_map/concatenate | solution.py:1606
  373.2 39.5 %plane_scatter13.1 = f32[256,384]{1,0:T(8,128)} custom-call(bf16[2,2,4,2,256,384]{5,4,3,2,1,0:T(8,128)(2,1)} %bitcast.522), custom_call_target="tpu_custom_call" | custom-call | tf_op jit(solution)/shard_map/plane_scatter13/pallas_call | solution.py:70
  421.1 4.1 convolution_bitcast_fusion.1
  425.2 3.3 multiply_reduce_fusion
  439.5 2.4 pad_maximum_fusion.1
  441.9 6.8 %copy.216 = bf16[2,1536,768]{2,1,0:T(8,128)(2,1)} copy(bf16[2,1536,768]{1,2,0:T(8,128)(2,1)} %pad_maximum_fusion.1) | data formatting | bytes 9437184 | tf_op jit(solution)/shard_map/concatenate | solution.py:1597
  448.7 30.4 %plane_scatter12.1 = f32[96,768]{1,0:T(8,128)} custom-call(bf16[2,2,4,2,96,768]{5,4,3,2,1,0:T(8,128)(2,1)} %bitcast.523), custom_call_target="tpu_custom_call" | custom-call | tf_op jit(solution)/shard_map/plane_scatter12/pallas_call | solution.py:70
  483.7 3.7 fusion.8
  487.4 18.0 %z_scatter11.1 = f32[128,1536]{1,0:T(8,128)} custom-call(bf16[4,128,1536]{2,1,0:T(8,128)(2,1)} %bitcast.533), custom_call_target="tpu_custom_call" | custom-call | tf_op jit(solution)/shard_map/z_scatter11/pallas_call | solution.py:70
  510.0 17.7 %small_sums.1 = (f32[16,2,8,128]{3,2,1,0:T(8,128)}, f32[8,128]{1,0:T(8,128)}, f32[8,8,128]{2,1,0:T(8,128)}) custom-call(f32[8,8,128]{2,1,0:T(8,128)} %pad.21.mod_ref, f32[16,8,128]{2,1,0:T(8,128)} %select_maximum_fusion.gain_ref), custom_call_target="tpu_custom_call" | custom-call | tf_op jit(solution)/shard_map/small_sums/pallas_call | solution.py:70
  534.1 16.0 %swap_back.1 = (bf16[2,64,1536]{2,1,0:T(8,128)(2,1)}, f32[2,64,1536]{2,1,0:T(8,128)}) custom-call(bf16[2,64,1536]{2,1,0:T(8,128)(2,1)} %bitcast.567, f32[2,64,1536]{2,1,0:T(8,128)} %bitcast.539), custom_call_target="tpu_custom_call" | custom-call | tf_op jit(solution)/shard_map/swap_back/pallas_call | solution.py:70
  (367 shorter events, 127.6 us)
Async XLA Ops:
  12.8 115.9 %copy-start.43 = (f32[64]{0:T(128)}, f32[64]{0:T(128)S(1)}, u32[]{:S(2)}) copy-start(f32[64]{0:T(128)S(1)} %get-tuple-element.179) | copy-start | bytes 772
  128.7 69.4 %copy-start.9 = (bf16[128,1536]{1,0:T(8,128)(2,1)S(1)}, bf16[128,1536]{1,0:T(8,128)(2,1)}, u32[]{:S(2)}) copy-start(bf16[128,1536]{1,0:T(8,128)(2,1)} %get-tuple-element.57) | copy-start | bytes 1179652
  128.7 75.4 %copy-start.37 = (bf16[3,256,128]{2,1,0:T(8,128)(2,1)S(1)}, bf16[3,256,128]{2,1,0:T(8,128)(2,1)}, u32[]{:S(2)}) copy-start(bf16[3,256,128]{2,1,0:T(8,128)(2,1)} %get-tuple-element.65) | copy-start | bytes 589828
  128.7 79.2 %copy-start.36 = (bf16[3,256,128]{2,1,0:T(8,128)(2,1)S(1)}, bf16[3,256,128]{2,1,0:T(8,128)(2,1)}, u32[]{:S(2)}) copy-start(bf16[3,256,128]{2,1,0:T(8,128)(2,1)} %get-tuple-element.66) | copy-start | bytes 589828
  128.7 83.1 %copy-start.35 = (f32[4,128,128]{2,1,0:T(8,128)S(1)}, f32[4,128,128]{2,1,0:T(8,128)}, u32[]{:S(2)}) copy-start(f32[4,128,128]{2,1,0:T(8,128)} %get-tuple-element.61) | copy-start | bytes 786436
  195.8 16.5 %copy-start.34 = (f32[4,128,128]{2,1,0:T(8,128)S(1)}, f32[4,128,128]{2,1,0:T(8,128)}, u32[]{:S(2)}) copy-start(f32[4,128,128]{2,1,0:T(8,128)} %get-tuple-element.67) | copy-start | bytes 786436
  195.8 17.9 %copy-start.33 = (f32[4,128,128]{2,1,0:T(8,128)S(1)}, f32[4,128,128]{2,1,0:T(8,128)}, u32[]{:S(2)}) copy-start(f32[4,128,128]{2,1,0:T(8,128)} %get-tuple-element.68) | copy-start | bytes 786436
  217.1 7.9 %copy-start.23 = (bf16[3,4,128,128]{3,2,1,0:T(8,128)(2,1)S(1)}, bf16[3,4,128,128]{3,2,1,0:T(8,128)(2,1)}, u32[]{:S(2)}) copy-start(bf16[3,4,128,128]{3,2,1,0:T(8,128)(2,1)} %get-tuple-element.60) | copy-start | bytes 1179652
  219.6 7.9 %copy-start.22 = (bf16[3,4,128,128]{3,2,1,0:T(8,128)(2,1)S(1)}, bf16[3,4,128,128]{3,2,1,0:T(8,128)(2,1)}, u32[]{:S(2)}) copy-start(bf16[3,4,128,128]{3,2,1,0:T(8,128)(2,1)} %get-tuple-element.64) | copy-start | bytes 1179652
  225.8 7.9 %copy-start.21 = (bf16[2,4,128,256]{3,2,1,0:T(8,128)(2,1)S(1)}, bf16[2,4,128,256]{3,2,1,0:T(8,128)(2,1)}, u32[]{:S(2)}) copy-start(bf16[2,4,128,256]{3,2,1,0:T(8,128)(2,1)} %get-tuple-element.80) | copy-start | bytes 1572868
  237.0 60.6 %copy-start.17 = (f32[3,4,128,128]{3,2,1,0:T(8,128)S(1)}, f32[3,4,128,128]{3,2,1,0:T(8,128)}, u32[]{:S(2)}) copy-start(f32[3,4,128,128]{3,2,1,0:T(8,128)} %get-tuple-element.58) | copy-start | bytes 2359300
  316.0 17.1 %copy-start.15 = (f32[512,6,64]{0,2,1:T(8,128)}, f32[512,6,64]{0,2,1:T(8,128)S(1)}, u32[]{:S(2)}) copy-start(f32[512,6,64]{0,2,1:T(8,128)S(1)} %fusion.70) | copy-start | bytes 2359300
  448.7 33.1 %copy-start.18 = (bf16[2,1536,128]{1,2,0:T(8,128)(2,1)S(1)}, bf16[2,1536,128]{1,2,0:T(8,128)(2,1)}, u32[]{:S(2)}) copy-start(bf16[2,1536,128]{1,2,0:T(8,128)(2,1)} %copy.232) | copy-start | bytes 2359300
  448.7 33.1 %copy-start.26 = (bf16[2,1536,64]{1,2,0:T(8,128)(2,1)S(1)}, bf16[2,1536,64]{1,2,0:T(8,128)(2,1)}, u32[]{:S(2)}) copy-start(bf16[2,1536,64]{1,2,0:T(8,128)(2,1)} %copy.233) | copy-start | bytes 1179652
  483.7 21.7 %copy-start.10 = (bf16[128,1536]{1,0:T(8,128)(2,1)S(1)}, bf16[128,1536]{1,0:T(8,128)(2,1)}, u32[]{:S(2)}) copy-start(bf16[128,1536]{1,0:T(8,128)(2,1)} %get-tuple-element.57) | copy-start | bytes 1179652
  483.7 21.7 %copy-start.40 = (f32[1536]{0:T(1024)S(1)}, f32[1536]{0:T(1024)}, u32[]{:S(2)}) copy-start(f32[1536]{0:T(1024)} %add_reduce_fusion) | copy-start | bytes 18436
  483.7 21.8 %copy-start.49 = (f32[128]{0:T(128)S(1)}, f32[128]{0:T(128)}, u32[]{:S(2)}) copy-start(f32[128]{0:T(128)} %add_rsqrt_fusion.3) | copy-start | bytes 1540
  487.4 19.7 %copy-start.38 = (f32[3,16,96]{2,0,1:T(4,128)S(1)}, f32[3,16,96]{2,0,1:T(4,128)}, u32[]{:S(2)}) copy-start(f32[3,16,96]{2,0,1:T(4,128)} %copy.206) | copy-start | bytes 55300
  487.4 20.4 %copy-start.20 = (f32[128,1536]{1,0:T(8,128)S(1)}, f32[128,1536]{1,0:T(8,128)}, u32[]{:S(2)}) copy-start(f32[128,1536]{1,0:T(8,128)} %get-tuple-element.56) | copy-start | bytes 2359300
  487.4 21.9 %copy-start.39 = (f32[3,1536]{1,0:T(4,128)S(1)}, f32[3,1536]{1,0:T(4,128)}, u32[]{:S(2)}) copy-start(f32[3,1536]{1,0:T(4,128)} %get-tuple-element.175) | copy-start | bytes 55300
  487.4 44.7 %copy-start.42 = (f32[16,2,64]{2,1,0:T(2,128)S(1)}, f32[16,2,64]{2,1,0:T(2,128)}, u32[]{:S(2)}) copy-start(f32[16,2,64]{2,1,0:T(2,128)} %slice.467) | copy-start | bytes 24580
  507.8 44.3 %copy-start.51 = (pred[2]{0:T(512)(128)(4,1)S(1)}, pred[2]{0:T(512)(128)(4,1)}, u32[]{:S(2)}) copy-start(pred[2]{0:T(512)(128)(4,1)} %iota_compare_fusion.4) | copy-start | bytes 10
  509.3 24.8 %copy-start.6 = (f32[128,1536]{1,0:T(8,128)}, f32[128,1536]{1,0:T(8,128)S(1)}, u32[]{:S(2)}) copy-start(f32[128,1536]{1,0:T(8,128)S(1)} %fusion.40) | copy-start | bytes 2359300
  509.3 43.8 %copy-start.19 = (bf16[64,1536]{1,0:T(8,128)(2,1)S(1)}, bf16[64,1536]{1,0:T(8,128)(2,1)}, u32[]{:S(2)}) copy-start(bf16[64,1536]{1,0:T(8,128)(2,1)} %dynamic-slice_bitcast_fusion.3) | copy-start | bytes 589828
  (30 other events, 56.4 us)
